TPU v7x, 256 devices: a whole 4x4x8 slice. The times are simulated.
256 devices in a mesh: gx: 8 (over x_hi, y), gy: 32 (over x_lo, z, core).
Axes of the slice: x: 4 (x_hi: 2, x_lo: 2; x = x_hi * 2 + x_lo), y: 4, z: 8, core: 2. Of those that a mesh axis runs over, the one named last changes fastest.
Arguments:
- features: bfloat16 [8, 32, 4, 512, 128], P('gx', 'gy')
- occupancy: int32 [8, 32, 4, 512], P('gx', 'gy'), may hold values 0 or 1
- counts: int32 [8, 32], P('gx', 'gy'), may hold values from 1 to 4, as said below
- kernel_map: int32 [8, 32, 4, 27], P('gx', 'gy'), may hold values from 0 to 16, as said below
- x_send: int32 [8, 32, 2, 2], P('gx', 'gy'), may hold values from 0 to 4, as said below
- y_send: int32 [8, 32, 2, 4], P('gx', 'gy'), may hold values from 0 to 8, as said below
- weight: bfloat16 [27, 128, 128], replicated, may hold values from -0.109375 to 0.109375
- norm_gain: float32 [128], replicated, may hold values from 0.5 to 1.5
- norm_shift: float32 [128], replicated, may hold values from -3 to 3
- cotangent: bfloat16 [8, 32, 4, 512, 128], P('gx', 'gy'), may hold values from -6 to 6
Outputs:
- activations: bfloat16 [8, 32, 4, 512, 128], P('gx', 'gy')
- features_grad: bfloat16 [8, 32, 4, 512, 128], P('gx', 'gy')
- weight_grad: float32 [27, 128, 128], replicated
- gain_grad: float32 [128], replicated
- shift_grad: float32 [128], replicated
Inputs may be any that keep to these rules, and one draw needn't show every extreme that they name: `counts`: slots at or past a tile's count are empty; some tile is full. `kernel_map`: rows are numbered as in the brick table; 16 stands for an empty neighbour, and so does every tap of an empty slot. `x_send`: listed slots are live and distinct, in increasing order, followed by 4 as padding. `y_send`: entries index the first 8 rows of the sender's brick table, distinct, followed by 4 + 2 * 2 as padding.
All inputs are finite; a program needn't handle non-finite values. No bound on the sum of `occupancy` on one device may be relied on, other than what follows from the above.
Results may differ from a plain program's by a relative error of at most 0.0049.
Values may be sent and summed in bfloat16 or wider, within the bound.
No kernel may reach another device: no remote copies, remote signals or barrier semaphores. Data moves between devices by JAX's collectives and lax.ppermute only.
A program may use at most 192 MiB of HBM per device.

v0:
```python
import jax
import jax.numpy as jnp
from jax import lax
from jax.sharding import PartitionSpec as P

EDGE = 8


EPSILON = 1e-05


def with_halo(value, sides, width):
    for axis, dim in sides:
        size, length = (lax.axis_size(axis), value.shape[dim])
        up = [(i, (i + 1) % size) for i in range(size - 1)]
        down = [(j, i) for i, j in up]
        last = lax.slice_in_dim(value, length - width, length, axis=dim)
        initial = lax.slice_in_dim(value, 0, width, axis=dim)
        before = lax.ppermute(last, axis, up)
        after = lax.ppermute(initial, axis, down)
        value = jnp.concatenate([before, value, after], axis=dim)
    return value


def span_of(offset, length):
    if offset < 0:
        return (length - 1, length)
    if offset == 0:
        return (0, length)
    return (0, 1)


def assemble(bricks_table, row_map):
    length = bricks_table.shape[1]
    planes = []
    for move_x in (-1, 0, 1):
        row_parts = []
        for move_y in (-1, 0, 1):
            cell_parts = []
            for move_z in (-1, 0, 1):
                tap_index = 9 * (move_x + 1) + 3 * (move_y + 1) + move_z + 1
                bounds = [span_of(move_x, length), span_of(move_y, length), span_of(move_z, length)]
                chosen = jnp.take(bricks_table, row_map[:, tap_index], axis=0)
                cell_parts.append(
                    chosen[
                        :,
                        bounds[0][0] : bounds[0][1],
                        bounds[1][0] : bounds[1][1],
                        bounds[2][0] : bounds[2][1],
                        :,
                    ]
                )
            row_parts.append(jnp.concatenate(cell_parts, axis=3))
        planes.append(jnp.concatenate(row_parts, axis=2))
    return jnp.concatenate(planes, axis=1)


def tap_columns(padded, move_x, sign):
    length = padded.shape[1] - 2
    pieces = []
    for move_y in (-1, 0, 1):
        for move_z in (-1, 0, 1):
            anchor = [1 + sign * move_x, 1 + sign * move_y, 1 + sign * move_z]
            section = padded[
                :,
                anchor[0] : anchor[0] + length,
                anchor[1] : anchor[1] + length,
                anchor[2] : anchor[2] + length,
                :,
            ]
            pieces.append(section)
    stacked = jnp.concatenate(pieces, axis=-1)
    return stacked.reshape(-1, stacked.shape[-1])


def forward_conv(padded, weight):
    channels = weight.shape[1]
    summed = None
    for move_x in (-1, 0, 1):
        first = 9 * (move_x + 1)
        block = weight[first : first + 9].reshape(9 * channels, weight.shape[2])
        product = jnp.dot(tap_columns(padded, move_x, 1), block, preferred_element_type=jnp.float32)
        summed = product if summed is None else summed + product
    return summed


def transposed_conv(padded, weight):
    outputs = weight.shape[2]
    summed = None
    for move_x in (-1, 0, 1):
        first = 9 * (move_x + 1)
        block = jnp.transpose(weight[first : first + 9], (0, 2, 1)).reshape(
            9 * outputs, weight.shape[1]
        )
        product = jnp.dot(
            tap_columns(padded, move_x, -1), block, preferred_element_type=jnp.float32
        )
        summed = product if summed is None else summed + product
    return summed


def weight_terms(padded, grad_rows):
    channels = padded.shape[-1]
    terms = []
    for move_x in (-1, 0, 1):
        product = lax.dot_general(
            tap_columns(padded, move_x, 1),
            grad_rows,
            (((0,), (0,)), ((), ())),
            preferred_element_type=jnp.float32,
        )
        terms.append(product.reshape(9, channels, grad_rows.shape[1]))
    return jnp.concatenate(terms, axis=0)


def incoming_rows(arrived):
    from_lower = arrived[0]
    from_upper = arrived[3]
    return (from_lower, from_upper)


def extend_x(bricks, sends_x, move_rows):
    blank_row = jnp.zeros((1,) + bricks.shape[1:], bricks.dtype)
    chosen = jnp.take(jnp.concatenate((bricks, blank_row), axis=0), sends_x, axis=0)
    arrived = move_rows(chosen)
    from_lower, from_upper = incoming_rows(arrived)
    return jnp.concatenate((bricks, from_lower, from_upper), axis=0)


def extend_y(x_table, sends_y, move_rows):
    blank_row = jnp.zeros((1,) + x_table.shape[1:], x_table.dtype)
    chosen = jnp.take(jnp.concatenate((x_table, blank_row), axis=0), sends_y, axis=0)
    arrived = move_rows(chosen)
    from_lower, from_upper = incoming_rows(arrived)
    return jnp.concatenate((from_lower, from_upper), axis=0)


def build_table(bricks, sends_x, sends_y, move_x_rows, move_y_rows):
    x_table = extend_x(bricks, sends_x, move_x_rows)
    y_rows = extend_y(x_table, sends_y, move_y_rows)
    blank_row = jnp.zeros((1,) + bricks.shape[1:], bricks.dtype)
    return jnp.concatenate((x_table, y_rows, blank_row), axis=0)


def forward_x_rows(outgoing):
    return with_halo(outgoing, (("gx", 0),), 1)


def forward_y_rows(outgoing):
    return with_halo(outgoing, (("gy", 0),), 1)


def shards(
    features,
    occupancy,
    counts,
    kernel_map,
    x_send,
    y_send,
    weight,
    norm_gain,
    norm_shift,
    cotangent,
):
    nbricks, voxels, channels = (features.shape[2], features.shape[3], features.shape[4])
    length = EDGE
    slot_index = jnp.arange(nbricks, dtype=jnp.int32)
    live_mask = (
        occupancy[0, 0].astype(jnp.float32)
        * (slot_index < counts[0, 0])[:, None].astype(jnp.float32)
    ).reshape(-1, 1)
    inputs = features[0, 0].reshape(-1, channels) * live_mask.astype(jnp.bfloat16)
    row_map = kernel_map[0, 0]
    sends_x = x_send[0, 0]
    sends_y = y_send[0, 0]
    input_table = build_table(
        inputs.reshape(nbricks, length, length, length, channels),
        sends_x,
        sends_y,
        forward_x_rows,
        forward_y_rows,
    )
    padded_in = assemble(input_table, row_map)
    conv_out = forward_conv(padded_in, weight)
    live_count, first_sum, second_sum = lax.psum(
        (
            jnp.sum(live_mask),
            jnp.sum(conv_out * live_mask, axis=0),
            jnp.sum(conv_out * conv_out * live_mask, axis=0),
        ),
        ("gx", "gy"),
    )
    channel_mean = first_sum / live_count
    variance = second_sum / live_count - channel_mean * channel_mean
    inverse_std = lax.rsqrt(variance + EPSILON)
    normed = (conv_out - channel_mean) * inverse_std
    pre_act = norm_gain * normed + norm_shift
    sigmoid_pre = jax.nn.sigmoid(pre_act)
    activations = (pre_act * sigmoid_pre * live_mask).astype(jnp.bfloat16)
    grad_act = (
        cotangent[0, 0].reshape(-1, channels).astype(jnp.float32)
        * live_mask
        * sigmoid_pre
        * (1.0 + pre_act * (1.0 - sigmoid_pre))
    )
    sum_grad, sum_cross = lax.psum(
        (jnp.sum(grad_act, axis=0), jnp.sum(grad_act * normed, axis=0)), ("gx", "gy")
    )
    grad_conv = (
        norm_gain
        * inverse_std
        * (grad_act - (sum_grad + normed * sum_cross) / live_count)
        * live_mask
    ).astype(jnp.bfloat16)
    weight_total = lax.psum(weight_terms(padded_in, grad_conv), ("gx", "gy"))

    def again_x_rows(outgoing):
        return with_halo(outgoing, (("gx", 0),), 1)

    def again_y_rows(outgoing):
        return with_halo(outgoing, (("gy", 0),), 1)

    grad_table = build_table(
        grad_conv.reshape(nbricks, length, length, length, channels),
        sends_x,
        sends_y,
        again_x_rows,
        again_y_rows,
    )
    input_grad = transposed_conv(assemble(grad_table, row_map), weight)
    grad_scale = lax.rsqrt(live_count)
    features_grad = (
        (input_grad * live_mask).astype(jnp.bfloat16).reshape(1, 1, nbricks, voxels, channels)
    )
    return (
        activations.reshape(1, 1, nbricks, voxels, channels),
        features_grad,
        weight_total * grad_scale,
        sum_cross * grad_scale,
        sum_grad * grad_scale,
    )


def solution(mesh):
    placed = (
        P("gx", "gy", None, None, None),
        P("gx", "gy", None, None),
        P("gx", "gy"),
        P("gx", "gy", None, None),
        P("gx", "gy", None, None),
        P("gx", "gy", None, None),
        P(),
        P(),
        P(),
        P("gx", "gy", None, None, None),
    )
    return jax.shard_map(
        shards,
        mesh=mesh,
        in_specs=placed,
        out_specs=(P("gx", "gy", None, None, None), P("gx", "gy", None, None, None), P(), P(), P()),
        check_vma=False,
    )
```

profile of v0, /device:TPU:1, one launch (start us, length us, event | category | flops | bytes accessed | tf_op | source)
XLA Modules:
  0.0 668.5 jit_solution(9959585387578377028)
XLA Ops:
  15.2 4.0 collective-permute-start
  44.4 2.6 slice_bitcast_fusion
  49.6 2.0 gather_fusion.1
  53.6 4.4 collective-permute-start.2
  58.6 1.8 copy.24
  60.5 1.8 copy.25
  63.2 1.9 collective-permute-start.3
  66.4 7.5 %collective-permute-done.3 = bf16[1,4,8,8,8,128]{5,4,3,2,1,0:T(8,128)(2,1)S(1)} collective-permute-done((bf16[1,4,8,8,8,128]{5,4,3,2,1,0:T(8,128)(2,1)}, bf16[1,4,8,8,8,128]{5,4,3,2,1,0:T(8,128)(2,1)S(1)}, u32[]{:S(2)}, u32[]{:S(2)}) %collective-permute-start.3) | collective-permute-done | bytes 524320 | tf_op jit(solution)/shard_map/ppermute | solution.py:20
  91.6 1.7 gather_fusion.27
  93.3 1.7 gather_fusion.21
  95.0 1.7 gather_fusion.28
  117.0 3.2 maximum_maximum_fusion.5
  120.2 3.1 maximum_maximum_fusion.1
  132.5 6.7 %copy.29 = bf16[1152,2048]{1,0:T(8,128)(2,1)} copy(bf16[1152,2048]{0,1:T(8,128)(2,1)} %bitcast.41) | data formatting | bytes 9437184 | tf_op jit(solution)/shard_map/dot_general | solution.py:106
  139.2 1.9 slice_dynamic-update-slice_fusion.38
  141.2 2.3 slice_dynamic-update-slice_fusion.37
  143.5 2.2 slice_dynamic-update-slice_fusion.36
  156.8 1.7 gather_fusion.7
  158.6 1.7 gather_fusion.5
  173.9 2.0 maximum_maximum_fusion
  178.0 2.2 copy-done
  180.2 6.9 %copy.28 = bf16[1152,2048]{1,0:T(8,128)(2,1)} copy(bf16[1152,2048]{0,1:T(8,128)(2,1)} %bitcast.39) | data formatting | bytes 9437184 | tf_op jit(solution)/shard_map/dot_general | solution.py:106
  187.1 3.8 fusion.21
  190.9 3.8 convolution_add_fusion.3
  194.7 3.8 multiply_reduce_fusion.1
  198.5 83.4 %all-reduce.3 = (f32[128]{0:T(128)S(1)}, f32[]{:T(128)}, f32[128]{0:T(128)S(1)}) all-reduce(f32[128]{0:T(128)S(1)} %get-tuple-element.9, f32[]{:T(128)} %multiply_reduce_fusion.3, f32[128]{0:T(128)S(1)} %get-tuple-element.8), channel_id=1, replica_groups=mesh['gx'=8,'gy'=32] {'gx','gy'}, use_global_device_ids=true, to_apply=%region_1.0 | all-reduce | flops 257 | bytes 2056 | tf_op jit(solution)/shard_map/psum | solution.py:185
  284.8 73.3 %all-reduce.2 = (f32[128]{0:T(128)S(1)}, f32[128]{0:T(128)S(1)}) all-reduce(f32[128]{0:T(128)S(1)} %get-tuple-element.11, f32[128]{0:T(128)S(1)} %get-tuple-element.10), channel_id=1, replica_groups=mesh['gx'=8,'gy'=32] {'gx','gy'}, use_global_device_ids=true, to_apply=%region_9.13 | all-reduce | flops 256 | bytes 2048 | tf_op jit(solution)/shard_map/psum | solution.py:206
  359.3 3.9 fusion.8
  364.6 6.7 %copy.27 = bf16[1152,2048]{1,0:T(8,128)(2,1)} copy(bf16[1152,2048]{0,1:T(8,128)(2,1)} %bitcast.103) | data formatting | bytes 9437184 | tf_op jit(solution)/shard_map/dot_general | solution.py:106
  371.3 3.7 fusion.12
  378.4 2.8 collective-permute-start.4
  384.5 1.7 collective-permute-done.4
  386.2 3.8 collective-permute-done.5
  392.9 5.4 collective-permute-start.6
  398.4 2.1 collective-permute-start.7
  400.6 4.1 collective-permute-done.6
  405.9 3.2 collective-permute-done.7
  415.4 1.6 gather_fusion.53
  423.1 1.6 gather_fusion.54
  430.8 1.6 gather_fusion.55
  438.5 1.6 gather_fusion.43
  441.5 1.7 gather_fusion.41
  464.1 1.6 maximum_maximum_fusion.7
  465.8 2.0 maximum_maximum_fusion.3
  479.6 3.3 maximum_maximum_fusion.2
  488.3 2.3 fusion.1
  490.6 167.9 %all-reduce.6.cloned.1.call-done = f32[27,128,128]{2,1,0:T(8,128)} async-done(((f32[27,128,128]{2,1,0:T(8,128)}), f32[27,128,128]{2,1,0:T(8,128)}) %all-reduce.6.cloned.1.call-update) | async-done | bytes 1769488 | tf_op jit(solution)/shard_map/psum | solution.py:215
  658.5 2.9 broadcast_multiply_fusion
  (422 shorter events, 192.6 us)
Async XLA Ops:
  7.2 651.3 %all-reduce.6.cloned.1.call-start = ((), (), s32[]{:S(2)}) async-start(), calls=%async_computation | async-start | bytes 3538944 | tf_op jit(solution)/shard_map/psum | solution.py:215
  10.3 10.9 %copy-start.2 = (s32[1,1,4,27]{3,2,1,0:T(4,128)S(1)}, s32[1,1,4,27]{3,2,1,0:T(4,128)}, u32[]{:S(2)}) copy-start(s32[1,1,4,27]{3,2,1,0:T(4,128)} %param.19) | copy-start | bytes 1300
  10.3 20.3 %copy-start.29 = (s32[1,1,4,512]{3,2,1,0:T(4,128)S(1)}, s32[1,1,4,512]{3,2,1,0:T(4,128)}, u32[]{:S(2)}) copy-start(s32[1,1,4,512]{3,2,1,0:T(4,128)} %param.17) | copy-start | bytes 24580
  15.2 31.8 %collective-permute-start = (bf16[1,2,8,8,8,128]{5,4,3,2,1,0:T(8,128)(2,1)}, bf16[1,2,8,8,8,128]{5,4,3,2,1,0:T(8,128)(2,1)S(1)}, u32[]{:S(2)}, u32[]{:S(2)}) collective-permute-start(bf16[1,2,8,8,8,128]{5,4,3,2,1,0:T(8,128)(2,1)} %get-tuple-element.68), channel_id=1, source_target_pairs={{0,32},{32,64},{64,96},{96,128},{128,160},{160,192},{192,224},{1,3... | collective-permute-start | bytes 786440 | tf_op jit(solution)/shard_map/ppermute | solution.py:19
  19.2 27.7 %collective-permute-start.1 = (bf16[1,2,8,8,8,128]{5,4,3,2,1,0:T(8,128)(2,1)}, bf16[1,2,8,8,8,128]{5,4,3,2,1,0:T(8,128)(2,1)S(1)}, u32[]{:S(2)}, u32[]{:S(2)}) collective-permute-start(bf16[1,2,8,8,8,128]{5,4,3,2,1,0:T(8,128)(2,1)} %get-tuple-element.67), channel_id=1, source_target_pairs={{32,0},{64,32},{96,64},{128,96},{160,128},{192,160},{224,192},{33,... | collective-permute-start | bytes 786440 | tf_op jit(solution)/shard_map/ppermute | solution.py:20
  31.3 20.3 %copy-start.32 = (s32[1024]{0:T(1024)}, s32[1024]{0:T(1024)S(1)}, u32[]{:S(2)}) copy-start(s32[1024]{0:T(1024)S(1)} %pad_clamp_fusion.27) | copy-start | bytes 12292
  51.7 13.4 %copy-start.17 = (bf16[1,2,8,8,8,128]{5,4,3,2,1,0:T(8,128)(2,1)S(1)}, bf16[1,2,8,8,8,128]{5,4,3,2,1,0:T(8,128)(2,1)}, u32[]{:S(2)}) copy-start(bf16[1,2,8,8,8,128]{5,4,3,2,1,0:T(8,128)(2,1)} %copy-done.16) | copy-start | bytes 786436
  52.5 12.6 %copy-start.19 = (bf16[1,2,8,8,8,128]{5,4,3,2,1,0:T(8,128)(2,1)S(1)}, bf16[1,2,8,8,8,128]{5,4,3,2,1,0:T(8,128)(2,1)}, u32[]{:S(2)}) copy-start(bf16[1,2,8,8,8,128]{5,4,3,2,1,0:T(8,128)(2,1)} %copy-done.18) | copy-start | bytes 786436
  53.6 11.6 %collective-permute-start.2 = (bf16[1,4,8,8,8,128]{5,4,3,2,1,0:T(8,128)(2,1)}, bf16[1,4,8,8,8,128]{5,4,3,2,1,0:T(8,128)(2,1)}, u32[]{:S(2)}, u32[]{:S(2)}) collective-permute-start(bf16[1,4,8,8,8,128]{5,4,3,2,1,0:T(8,128)(2,1)} %get-tuple-element.54), channel_id=1, source_target_pairs={{0,1},{1,2},{2,3},{3,4},{4,5},{5,6},{6,7},{7,8},{8,9},{9,10},{10,1... | collective-permute-start | bytes 1572872 | tf_op jit(solution)/shard_map/ppermute | solution.py:19
  63.2 10.7 %collective-permute-start.3 = (bf16[1,4,8,8,8,128]{5,4,3,2,1,0:T(8,128)(2,1)}, bf16[1,4,8,8,8,128]{5,4,3,2,1,0:T(8,128)(2,1)S(1)}, u32[]{:S(2)}, u32[]{:S(2)}) collective-permute-start(bf16[1,4,8,8,8,128]{5,4,3,2,1,0:T(8,128)(2,1)} %get-tuple-element.53), channel_id=1, source_target_pairs={{1,0},{2,1},{3,2},{4,3},{5,4},{6,5},{7,6},{8,7},{9,8},{10,9},{11,1... | collective-permute-start | bytes 1572872 | tf_op jit(solution)/shard_map/ppermute | solution.py:20
  95.0 16.4 %copy-start.33 = (pred[4]{0:T(512)(128)(4,1)S(1)}, pred[4]{0:T(512)(128)(4,1)}, u32[]{:S(2)}) copy-start(pred[4]{0:T(512)(128)(4,1)} %get-tuple-element.95) | copy-start | bytes 16
  104.8 18.5 %copy-start.12 = (bf16[4,8,1,8,128]{4,3,2,1,0:T(8,128)(2,1)}, bf16[4,8,1,8,128]{4,3,2,1,0:T(8,128)(2,1)S(1)}, u32[]{:S(2)}) copy-start(bf16[4,8,1,8,128]{4,3,2,1,0:T(8,128)(2,1)S(1)} %slice_select_fusion.5) | copy-start | bytes 196612
  105.7 17.6 %copy-start.14 = (bf16[4,8,1,8,128]{4,3,2,1,0:T(8,128)(2,1)}, bf16[4,8,1,8,128]{4,3,2,1,0:T(8,128)(2,1)S(1)}, u32[]{:S(2)}) copy-start(bf16[4,8,1,8,128]{4,3,2,1,0:T(8,128)(2,1)S(1)} %slice_select_fusion.6) | copy-start | bytes 196612
  106.7 16.6 %copy-start.21 = (bf16[4,8,1,1,128]{4,3,2,1,0:T(2,128)(2,1)}, bf16[4,8,1,1,128]{4,3,2,1,0:T(2,128)(2,1)S(1)}, u32[]{:S(2)}) copy-start(bf16[4,8,1,1,128]{4,3,2,1,0:T(2,128)(2,1)S(1)} %broadcast_select_fusion.17) | copy-start | bytes 24580
  107.6 15.7 %copy-start.23 = (bf16[4,8,1,1,128]{4,3,2,1,0:T(2,128)(2,1)}, bf16[4,8,1,1,128]{4,3,2,1,0:T(2,128)(2,1)S(1)}, u32[]{:S(2)}) copy-start(bf16[4,8,1,1,128]{4,3,2,1,0:T(2,128)(2,1)S(1)} %broadcast_select_fusion.19) | copy-start | bytes 24580
  108.6 14.8 %copy-start.25 = (bf16[4,8,1,1,128]{4,3,2,1,0:T(2,128)(2,1)}, bf16[4,8,1,1,128]{4,3,2,1,0:T(2,128)(2,1)S(1)}, u32[]{:S(2)}) copy-start(bf16[4,8,1,1,128]{4,3,2,1,0:T(2,128)(2,1)S(1)} %broadcast_select_fusion.21) | copy-start | bytes 24580
  109.5 13.8 %copy-start.27 = (bf16[4,8,1,1,128]{4,3,2,1,0:T(2,128)(2,1)}, bf16[4,8,1,1,128]{4,3,2,1,0:T(2,128)(2,1)S(1)}, u32[]{:S(2)}) copy-start(bf16[4,8,1,1,128]{4,3,2,1,0:T(2,128)(2,1)S(1)} %broadcast_select_fusion.15) | copy-start | bytes 24580
  156.8 11.1 %copy-start.49 = (pred[4]{0:T(512)(128)(4,1)S(1)}, pred[4]{0:T(512)(128)(4,1)}, u32[]{:S(2)}) copy-start(pred[4]{0:T(512)(128)(4,1)} %get-tuple-element.119) | copy-start | bytes 16
  158.5 11.3 %copy-start.47 = (pred[4]{0:T(512)(128)(4,1)S(1)}, pred[4]{0:T(512)(128)(4,1)}, u32[]{:S(2)}) copy-start(pred[4]{0:T(512)(128)(4,1)} %get-tuple-element.120) | copy-start | bytes 16
  158.5 12.2 %copy-start.65 = (pred[4]{0:T(512)(128)(4,1)S(1)}, pred[4]{0:T(512)(128)(4,1)}, u32[]{:S(2)}) copy-start(pred[4]{0:T(512)(128)(4,1)} %get-tuple-element.122) | copy-start | bytes 16
  158.5 13.0 %copy-start.57 = (pred[4]{0:T(512)(128)(4,1)S(1)}, pred[4]{0:T(512)(128)(4,1)}, u32[]{:S(2)}) copy-start(pred[4]{0:T(512)(128)(4,1)} %get-tuple-element.117) | copy-start | bytes 16
  158.5 13.8 %copy-start.61 = (pred[4]{0:T(512)(128)(4,1)S(1)}, pred[4]{0:T(512)(128)(4,1)}, u32[]{:S(2)}) copy-start(pred[4]{0:T(512)(128)(4,1)} %get-tuple-element.121) | copy-start | bytes 16
  158.5 14.5 %copy-start.63 = (pred[4]{0:T(512)(128)(4,1)S(1)}, pred[4]{0:T(512)(128)(4,1)}, u32[]{:S(2)}) copy-start(pred[4]{0:T(512)(128)(4,1)} %get-tuple-element.123) | copy-start | bytes 16
  158.5 15.3 %copy-start.13 = (bf16[4,8,1,8,128]{4,3,2,1,0:T(8,128)(2,1)S(1)}, bf16[4,8,1,8,128]{4,3,2,1,0:T(8,128)(2,1)}, u32[]{:S(2)}) copy-start(bf16[4,8,1,8,128]{4,3,2,1,0:T(8,128)(2,1)} %copy-done.12) | copy-start | bytes 196612
  158.5 15.3 %copy-start.15 = (bf16[4,8,1,8,128]{4,3,2,1,0:T(8,128)(2,1)S(1)}, bf16[4,8,1,8,128]{4,3,2,1,0:T(8,128)(2,1)}, u32[]{:S(2)}) copy-start(bf16[4,8,1,8,128]{4,3,2,1,0:T(8,128)(2,1)} %copy-done.14) | copy-start | bytes 196612
  158.5 15.3 %copy-start.22 = (bf16[4,8,1,1,128]{4,3,2,1,0:T(2,128)(2,1)S(1)}, bf16[4,8,1,1,128]{4,3,2,1,0:T(2,128)(2,1)}, u32[]{:S(2)}) copy-start(bf16[4,8,1,1,128]{4,3,2,1,0:T(2,128)(2,1)} %copy-done.21) | copy-start | bytes 24580
  158.5 15.3 %copy-start.24 = (bf16[4,8,1,1,128]{4,3,2,1,0:T(2,128)(2,1)S(1)}, bf16[4,8,1,1,128]{4,3,2,1,0:T(2,128)(2,1)}, u32[]{:S(2)}) copy-start(bf16[4,8,1,1,128]{4,3,2,1,0:T(2,128)(2,1)} %copy-done.23) | copy-start | bytes 24580
  158.6 15.3 %copy-start.26 = (bf16[4,8,1,1,128]{4,3,2,1,0:T(2,128)(2,1)S(1)}, bf16[4,8,1,1,128]{4,3,2,1,0:T(2,128)(2,1)}, u32[]{:S(2)}) copy-start(bf16[4,8,1,1,128]{4,3,2,1,0:T(2,128)(2,1)} %copy-done.25) | copy-start | bytes 24580
  158.6 15.3 %copy-start.28 = (bf16[4,8,1,1,128]{4,3,2,1,0:T(2,128)(2,1)S(1)}, bf16[4,8,1,1,128]{4,3,2,1,0:T(2,128)(2,1)}, u32[]{:S(2)}) copy-start(bf16[4,8,1,1,128]{4,3,2,1,0:T(2,128)(2,1)} %copy-done.27) | copy-start | bytes 24580
  194.7 87.9 %copy-start.69 = (f32[128]{0:T(128)S(1)}, f32[128]{0:T(128)}, u32[]{:S(2)}) copy-start(f32[128]{0:T(128)} %param.23) | copy-start | bytes 1540
  194.7 88.6 %copy-start.20 = (bf16[1,1,4,512,128]{4,3,2,1,0:T(8,128)(2,1)S(1)}, bf16[1,1,4,512,128]{4,3,2,1,0:T(8,128)(2,1)}, u32[]{:S(2)}) copy-start(bf16[1,1,4,512,128]{4,3,2,1,0:T(8,128)(2,1)} %param.25) | copy-start | bytes 1572868
  194.7 88.6 %copy-start.73 = (f32[128]{0:T(128)S(1)}, f32[128]{0:T(128)}, u32[]{:S(2)}) copy-start(f32[128]{0:T(128)} %param.24) | copy-start | bytes 1540
  377.2 12.9 %copy-start.10 = (bf16[1,8,8,8,128]{4,3,2,1,0:T(8,128)(2,1)S(1)}, bf16[1,8,8,8,128]{4,3,2,1,0:T(8,128)(2,1)}, u32[]{:S(2)}) copy-start(bf16[1,8,8,8,128]{4,3,2,1,0:T(8,128)(2,1)} %copy-done.9) | copy-start | bytes 393220
  378.4 7.8 %collective-permute-start.4 = (bf16[1,2,8,8,8,128]{5,4,3,2,1,0:T(8,128)(2,1)S(1)}, bf16[1,2,8,8,8,128]{5,4,3,2,1,0:T(8,128)(2,1)S(1)}, u32[]{:S(2)}, u32[]{:S(2)}) collective-permute-start(bf16[1,2,8,8,8,128]{5,4,3,2,1,0:T(8,128)(2,1)S(1)} %get-tuple-element.66), channel_id=1, source_target_pairs={{0,32},{32,64},{64,96},{96,128},{128,160},{160,192},{192,224},{1,3... | collective-permute-start | bytes 786440 | tf_op jit(solution)/shard_map/ppermute | solution.py:19
  381.3 8.8 %collective-permute-start.5 = (bf16[1,2,8,8,8,128]{5,4,3,2,1,0:T(8,128)(2,1)S(1)}, bf16[1,2,8,8,8,128]{5,4,3,2,1,0:T(8,128)(2,1)S(1)}, u32[]{:S(2)}, u32[]{:S(2)}) collective-permute-start(bf16[1,2,8,8,8,128]{5,4,3,2,1,0:T(8,128)(2,1)S(1)} %get-tuple-element.65), channel_id=1, source_target_pairs={{32,0},{64,32},{96,64},{128,96},{160,128},{192,160},{224,192},{33,... | collective-permute-start | bytes 786440 | tf_op jit(solution)/shard_map/ppermute | solution.py:20
  392.9 11.8 %collective-permute-start.6 = (bf16[1,4,8,8,8,128]{5,4,3,2,1,0:T(8,128)(2,1)}, bf16[1,4,8,8,8,128]{5,4,3,2,1,0:T(8,128)(2,1)}, u32[]{:S(2)}, u32[]{:S(2)}) collective-permute-start(bf16[1,4,8,8,8,128]{5,4,3,2,1,0:T(8,128)(2,1)} %get-tuple-element.52), channel_id=1, source_target_pairs={{0,1},{1,2},{2,3},{3,4},{4,5},{5,6},{6,7},{7,8},{8,9},{9,10},{10,1... | collective-permute-start | bytes 1572872 | tf_op jit(solution)/shard_map/ppermute | solution.py:19
  398.4 10.7 %collective-permute-start.7 = (bf16[1,4,8,8,8,128]{5,4,3,2,1,0:T(8,128)(2,1)}, bf16[1,4,8,8,8,128]{5,4,3,2,1,0:T(8,128)(2,1)S(1)}, u32[]{:S(2)}, u32[]{:S(2)}) collective-permute-start(bf16[1,4,8,8,8,128]{5,4,3,2,1,0:T(8,128)(2,1)} %get-tuple-element.51), channel_id=1, source_target_pairs={{1,0},{2,1},{3,2},{4,3},{5,4},{6,5},{7,6},{8,7},{9,8},{10,9},{11,1... | collective-permute-start | bytes 1572872 | tf_op jit(solution)/shard_map/ppermute | solution.py:20
  443.2 11.5 %copy-start.37 = (pred[4]{0:T(512)(128)(4,1)S(1)}, pred[4]{0:T(512)(128)(4,1)}, u32[]{:S(2)}) copy-start(pred[4]{0:T(512)(128)(4,1)} %get-tuple-element.101) | copy-start | bytes 16
  443.2 12.5 %copy-start.36 = (pred[4]{0:T(512)(128)(4,1)S(1)}, pred[4]{0:T(512)(128)(4,1)}, u32[]{:S(2)}) copy-start(pred[4]{0:T(512)(128)(4,1)} %get-tuple-element.105) | copy-start | bytes 16
  443.2 13.4 %copy-start.40 = (pred[4]{0:T(512)(128)(4,1)S(1)}, pred[4]{0:T(512)(128)(4,1)}, u32[]{:S(2)}) copy-start(pred[4]{0:T(512)(128)(4,1)} %get-tuple-element.107) | copy-start | bytes 16
  443.2 14.3 %copy-start.46 = (pred[4]{0:T(512)(128)(4,1)S(1)}, pred[4]{0:T(512)(128)(4,1)}, u32[]{:S(2)}) copy-start(pred[4]{0:T(512)(128)(4,1)} %get-tuple-element.118) | copy-start | bytes 16
  443.2 15.3 %copy-start.48 = (pred[4]{0:T(512)(128)(4,1)S(1)}, pred[4]{0:T(512)(128)(4,1)}, u32[]{:S(2)}) copy-start(pred[4]{0:T(512)(128)(4,1)} %get-tuple-element.120) | copy-start | bytes 16
  443.3 16.2 %copy-start.60 = (pred[4]{0:T(512)(128)(4,1)S(1)}, pred[4]{0:T(512)(128)(4,1)}, u32[]{:S(2)}) copy-start(pred[4]{0:T(512)(128)(4,1)} %get-tuple-element.116) | copy-start | bytes 16
  443.3 17.0 %copy-start.71 = (pred[4]{0:T(512)(128)(4,1)S(1)}, pred[4]{0:T(512)(128)(4,1)}, u32[]{:S(2)}) copy-start(pred[4]{0:T(512)(128)(4,1)} %compare_and_fusion.18) | copy-start | bytes 16
  443.3 17.7 %copy-start.66 = (pred[4]{0:T(512)(128)(4,1)S(1)}, pred[4]{0:T(512)(128)(4,1)}, u32[]{:S(2)}) copy-start(pred[4]{0:T(512)(128)(4,1)} %get-tuple-element.122) | copy-start | bytes 16
  443.3 18.5 %copy-start.58 = (pred[4]{0:T(512)(128)(4,1)S(1)}, pred[4]{0:T(512)(128)(4,1)}, u32[]{:S(2)}) copy-start(pred[4]{0:T(512)(128)(4,1)} %get-tuple-element.117) | copy-start | bytes 16
  443.3 19.3 %copy-start.62 = (pred[4]{0:T(512)(128)(4,1)S(1)}, pred[4]{0:T(512)(128)(4,1)}, u32[]{:S(2)}) copy-start(pred[4]{0:T(512)(128)(4,1)} %get-tuple-element.121) | copy-start | bytes 16
  443.3 20.0 %copy-start.64 = (pred[4]{0:T(512)(128)(4,1)S(1)}, pred[4]{0:T(512)(128)(4,1)}, u32[]{:S(2)}) copy-start(pred[4]{0:T(512)(128)(4,1)} %get-tuple-element.123) | copy-start | bytes 16
  (38 other events, 226.9 us)
Sparse Core Ops, SparseCore 0:
  398.5 259.9 all-reduce.5
where the time goes:
time: 679 us; the launch traced here: 668 us
  waiting for transfers between devices  188 us (28%)
  blocking collectives  157 us (23%)
  local copies, waits for them, and re-layouts  152 us (22%)
  other arithmetic  106 us (16%)
  matrix products  25.5 us (4%)
  starting transfers between devices  23.3 us (3%)
  between operations  17.2 us (3%)
    psum x1, waiting for transfers between devices, shards(): weight_total = lax.psum(weight_terms(padded_in, grad_conv), ('gx', 'gy'))  168 us
    psum x1, blocking collectives, shards(): lax.psum((jnp.sum(live_mask), jnp.sum(conv_out * live_mask, axis=0), jnp....  83.4 us
    gather x54, local copies, waits for them, and re-layouts, assemble(): chosen = jnp.take(bricks_table, row_map[:, tap_index], axis=0)  81.3 us
    psum x1, blocking collectives, shards(): lax.psum((jnp.sum(grad_act, axis=0), jnp.sum(grad_act * normed, axis=0)),...  73.3 us
    select_n x72, other arithmetic, assemble(): chosen = jnp.take(bricks_table, row_map[:, tap_index], axis=0)  45.6 us
    unnamed x208, local copies, waits for them, and re-layouts  29.8 us
    dot_general x3, local copies, waits for them, and re-layouts, weight_terms(): lax.dot_general(tap_columns(padded, move_x, 1), grad_rows, (((0,), (0,)),...  20.3 us
    ppermute x4, starting transfers between devices, with_halo(): before = lax.ppermute(last, axis, up)  16.7 us
  transfers between devices with their start and end apart: 9, of which 6 were waited for; matrix products, arithmetic and copies ran while one was open for 17% of the time, Pallas kernels for 0%

commit v1 on v0

v1 whole, which is shorter than its diff:
```python
import functools

import jax
import jax.numpy as jnp
from jax import lax
from jax.experimental import pallas as pl
from jax.experimental.pallas import tpu as pltpu
from jax.sharding import PartitionSpec as P

EDGE = 8
PLANE = 64
VOX = 512
CH = 128
SLOTS = 4
HX = 2
HY = 4
EPSILON = 1e-05
F32 = jnp.float32
BF16 = jnp.bfloat16

VM = pl.BlockSpec(memory_space=pltpu.VMEM)
SM = pl.BlockSpec(memory_space=pltpu.SMEM)
LIMIT = 56 * 1024 * 1024


def params():
    return pltpu.CompilerParams(vmem_limit_bytes=LIMIT)


def cost(flops, moved):
    return pl.CostEstimate(flops=flops, bytes_accessed=moved, transcendentals=0)


def shape(dims, kind):
    return jax.ShapeDtypeStruct(dims, kind)


def pick_x(sends_ref, own_ref, low_ref, high_ref):
    for side, out_ref in ((0, low_ref), (1, high_ref)):
        for k in range(HX):
            row = sends_ref[side, k]
            brick = own_ref[jnp.minimum(row, SLOTS - 1)]
            out_ref[k] = jnp.where(row < SLOTS, brick, jnp.zeros_like(brick))


def prepare_kernel(counts_ref, sends_ref, feat_ref, occ_ref, own_ref, mask_ref, low_ref, high_ref):
    for s in range(SLOTS):
        live = (s < counts_ref[0, 0]).astype(F32)
        for k in range(VOX // CH):
            row = occ_ref[s : s + 1, k * CH : (k + 1) * CH].astype(F32) * live
            column = jnp.transpose(jnp.broadcast_to(row, (CH, CH)))
            rows = pl.ds(k * CH, CH)
            mask_ref[s, rows, :] = column.astype(BF16)
            own_ref[s, rows, :] = (feat_ref[s, rows, :].astype(F32) * column).astype(BF16)
    pick_x(sends_ref, own_ref, low_ref, high_ref)


def prepare(counts, sends_x, features, occupancy):
    return pl.pallas_call(
        prepare_kernel,
        out_shape=(
            shape((SLOTS, VOX, CH), BF16),
            shape((SLOTS, VOX, CH), BF16),
            shape((HX, VOX, CH), BF16),
            shape((HX, VOX, CH), BF16),
        ),
        in_specs=[SM, SM, VM, VM],
        out_specs=(VM, VM, VM, VM),
        compiler_params=params(),
        cost_estimate=cost(1 << 20, 2 << 20),
        name="prepare",
    )(counts, sends_x, features, occupancy)


def pick_y_kernel(sends_ref, own_ref, xl_ref, xu_ref, low_ref, high_ref):
    for side, out_ref in ((0, low_ref), (1, high_ref)):
        for k in range(HY):
            row = sends_ref[side, k]

            @pl.when(row < SLOTS)
            def _():
                out_ref[k] = own_ref[jnp.minimum(row, SLOTS - 1)]

            @pl.when((row >= SLOTS) & (row < SLOTS + HX))
            def _():
                out_ref[k] = xl_ref[jnp.clip(row - SLOTS, 0, HX - 1)]

            @pl.when((row >= SLOTS + HX) & (row < SLOTS + 2 * HX))
            def _():
                out_ref[k] = xu_ref[jnp.clip(row - SLOTS - HX, 0, HX - 1)]

            @pl.when(row >= SLOTS + 2 * HX)
            def _():
                out_ref[k] = jnp.zeros((VOX, CH), BF16)


def pick_y(sends_y, own, xl, xu):
    return pl.pallas_call(
        pick_y_kernel,
        out_shape=(shape((HY, VOX, CH), BF16), shape((HY, VOX, CH), BF16)),
        in_specs=[SM, VM, VM, VM],
        out_specs=(VM, VM),
        compiler_params=params(),
        cost_estimate=cost(1 << 20, 2 << 20),
        name="pick_y",
    )(sends_y, own, xl, xu)


def neighbours(low, high, axis):
    size = lax.axis_size(axis)
    up = [(i, i + 1) for i in range(size - 1)]
    down = [(j, i) for i, j in up]
    return lax.ppermute(high, axis, up), lax.ppermute(low, axis, down)


def fill_columns(map_ref, slot, table_ref, x9_ref):
    sub = lax.broadcasted_iota(jnp.int32, (EDGE + 2, EDGE, CH), 1)
    for a in range(-1, EDGE + 1):
        move = -1 if a < 0 else (1 if a >= EDGE else 0)
        base = (a % EDGE) * PLANE
        spans = []
        for r in (-1, 0, 1):
            tap = 9 * (move + 1) + r + 1
            before = table_ref[map_ref[slot, tap], base + 48 : base + 64, :].astype(F32)[8:]
            middle = table_ref[map_ref[slot, tap + 3], base : base + 64, :].astype(F32)
            after = table_ref[map_ref[slot, tap + 6], base : base + 16, :].astype(F32)[:8]
            spans.append(jnp.concatenate((before, middle, after), axis=0).reshape(EDGE + 2, EDGE, CH))
        low, centre, high = spans
        down = pltpu.roll(jnp.where(sub == EDGE - 1, low, centre), 1, 1)
        up = pltpu.roll(jnp.where(sub == 0, high, centre), EDGE - 1, 1)
        for r, source in ((-1, down), (0, centre), (1, up)):
            for q in (-1, 0, 1):
                rows = source[q + 1 : q + 1 + EDGE].reshape(PLANE, CH).astype(BF16)
                lane = (3 * (q + 1) + r + 1) * CH
                x9_ref[(a + 1) * PLANE : (a + 2) * PLANE, lane : lane + CH] = rows


def conv_kernel(map_ref, own_ref, xl_ref, xu_ref, yl_ref, yu_ref, w_ref, mask_ref, *rest, forward):
    slot = pl.program_id(0)
    if forward:
        out_ref, x9_out, stat_ref, table_ref = rest
        x9_ref = x9_out.at[0]
    else:
        out_ref, table_ref, x9_ref = rest

    @pl.when(slot == 0)
    def _():
        start = 0
        for ref in (own_ref, xl_ref, xu_ref, yl_ref, yu_ref):
            table_ref[start : start + ref.shape[0]] = ref[...]
            start += ref.shape[0]
        table_ref[start] = jnp.zeros((VOX, CH), BF16)
        if forward:
            stat_ref[...] = jnp.zeros_like(stat_ref)

    fill_columns(map_ref, slot, table_ref, x9_ref)
    total = None
    for p in range(3):
        term = jnp.dot(
            x9_ref[p * PLANE : p * PLANE + VOX, :], w_ref[p], preferred_element_type=F32
        )
        total = term if total is None else total + term
    mask = mask_ref[0].astype(F32)
    masked = total * mask
    if forward:
        out_ref[0] = total
        stat_ref[0:1] += jnp.sum(masked, axis=0, keepdims=True)
        stat_ref[1:2] += jnp.sum(masked * total, axis=0, keepdims=True)
        stat_ref[2:3] += jnp.sum(mask, axis=0, keepdims=True)
    else:
        out_ref[0] = masked.astype(BF16)


def conv(row_map, own, xl, xu, yl, yu, weight, mask, forward):
    brick = pl.BlockSpec((1, VOX, CH), lambda s: (s, 0, 0))
    whole = lambda *dims: pl.BlockSpec(dims, lambda s: (0,) * len(dims))
    scratch = [pltpu.VMEM((17, VOX, CH), BF16)]
    if forward:
        out_shape = (
            shape((SLOTS, VOX, CH), F32),
            shape((SLOTS, 10 * PLANE, 9 * CH), BF16),
            shape((8, CH), F32),
        )
        out_specs = (brick, pl.BlockSpec((1, 10 * PLANE, 9 * CH), lambda s: (s, 0, 0)), whole(8, CH))
    else:
        out_shape = shape((SLOTS, VOX, CH), BF16)
        out_specs = brick
        scratch.append(pltpu.VMEM((10 * PLANE, 9 * CH), BF16))
    return pl.pallas_call(
        functools.partial(conv_kernel, forward=forward),
        grid=(SLOTS,),
        out_shape=out_shape,
        in_specs=[
            SM,
            whole(SLOTS, VOX, CH),
            whole(HX, VOX, CH),
            whole(HX, VOX, CH),
            whole(HY, VOX, CH),
            whole(HY, VOX, CH),
            whole(3, 9 * CH, CH),
            brick,
        ],
        out_specs=out_specs,
        scratch_shapes=scratch,
        compiler_params=params(),
        cost_estimate=cost(1811939328, 12 << 20),
        name="forward_conv" if forward else "transposed_conv",
    )(row_map, own, xl, xu, yl, yu, weight, mask)


def norm_terms(stats, gain, shift):
    count = stats[2:3]
    mean = stats[0:1] / count
    variance = stats[1:2] / count - mean * mean
    return count, mean, lax.rsqrt(variance + EPSILON)


def act_kernel(stat_ref, conv_ref, cot_ref, mask_ref, gain_ref, shift_ref, act_ref, ga_ref, g_ref, sum_ref, norm_ref):
    slot = pl.program_id(0)
    count, mean, inverse = norm_terms(jnp.sum(stat_ref[...], axis=0), None, None)

    @pl.when(slot == 0)
    def _():
        sum_ref[...] = jnp.zeros_like(sum_ref)
        norm_ref[...] = jnp.concatenate((mean, inverse, count, jnp.zeros((5, CH), F32)), axis=0)

    mask = mask_ref[0].astype(F32)
    normed = (conv_ref[0] - mean) * inverse
    pre = gain_ref[...] * normed + shift_ref[...]
    sig = jax.nn.sigmoid(pre)
    act_ref[0] = (pre * sig * mask).astype(BF16)
    ga = cot_ref[0].astype(F32) * mask * sig * (1.0 + pre * (1.0 - sig))
    ga_ref[0] = ga
    sum_ref[0:1] += jnp.sum(ga, axis=0, keepdims=True)
    sum_ref[1:2] += jnp.sum(ga * normed, axis=0, keepdims=True)
    nm = normed * mask
    for k in range(VOX // CH):
        rows = slice(k * CH, (k + 1) * CH)
        g_ref[0, 0:CH, rows] = jnp.transpose(ga[rows]).astype(BF16)
        g_ref[0, CH : 2 * CH, rows] = jnp.transpose(nm[rows]).astype(BF16)
        g_ref[0, 2 * CH : 2 * CH + 16, rows] = jnp.transpose(mask[rows])[0:16].astype(BF16)


def act(stats, conv_out, cotangent, mask, gain, shift):
    brick = pl.BlockSpec((1, VOX, CH), lambda s: (s, 0, 0))
    whole = lambda *dims: pl.BlockSpec(dims, lambda s: (0,) * len(dims))
    return pl.pallas_call(
        act_kernel,
        grid=(SLOTS,),
        out_shape=(
            shape((SLOTS, VOX, CH), BF16),
            shape((SLOTS, VOX, CH), F32),
            shape((SLOTS, 2 * CH + 16, VOX), BF16),
            shape((8, CH), F32),
            shape((8, CH), F32),
        ),
        in_specs=[whole(*stats.shape), brick, brick, brick, whole(1, CH), whole(1, CH)],
        out_specs=(
            brick,
            brick,
            pl.BlockSpec((1, 2 * CH + 16, VOX), lambda s: (s, 0, 0)),
            whole(8, CH),
            whole(8, CH),
        ),
        compiler_params=params(),
        cost_estimate=cost(8 << 20, 5 << 20),
        name="activation",
    )(stats, conv_out, cotangent, mask, gain, shift)


def wgrad_kernel(g_ref, x9_ref, out_ref):
    slot = pl.program_id(0)
    for p in range(3):
        term = jnp.dot(
            g_ref[0], x9_ref[0, p * PLANE : p * PLANE + VOX, :], preferred_element_type=F32
        )

        @pl.when(slot == 0)
        def _():
            out_ref[p] = term

        @pl.when(slot > 0)
        def _():
            out_ref[p] += term


def wgrad(g, x9):
    return pl.pallas_call(
        wgrad_kernel,
        grid=(SLOTS,),
        out_shape=shape((3, 2 * CH + 16, 9 * CH), F32),
        in_specs=[
            pl.BlockSpec((1, 2 * CH + 16, VOX), lambda s: (s, 0, 0)),
            pl.BlockSpec((1, 10 * PLANE, 9 * CH), lambda s: (s, 0, 0)),
        ],
        out_specs=pl.BlockSpec((3, 2 * CH + 16, 9 * CH), lambda s: (0, 0, 0)),
        compiler_params=params(),
        cost_estimate=cost(2 * 1811939328, 12 << 20),
        name="weight_terms",
    )(g, x9)


def grad_kernel(sends_ref, sum_ref, norm_ref, gain_ref, conv_ref, ga_ref, mask_ref, out_ref, low_ref, high_ref, tot_ref):
    totals = jnp.sum(sum_ref[...], axis=0)
    mean, inverse, count = norm_ref[0:1], norm_ref[1:2], norm_ref[2:3]
    tot_ref[...] = totals
    factor = gain_ref[...] * inverse
    for s in range(SLOTS):
        normed = (conv_ref[s] - mean) * inverse
        inner = ga_ref[s] - (totals[0:1] + normed * totals[1:2]) / count
        out_ref[s] = (factor * inner * mask_ref[s].astype(F32)).astype(BF16)
    pick_x(sends_ref, out_ref, low_ref, high_ref)


def grad(sends_x, sums, norm, gain, conv_out, ga, mask):
    return pl.pallas_call(
        grad_kernel,
        out_shape=(
            shape((SLOTS, VOX, CH), BF16),
            shape((HX, VOX, CH), BF16),
            shape((HX, VOX, CH), BF16),
            shape((8, CH), F32),
        ),
        in_specs=[SM] + [VM] * 6,
        out_specs=(VM,) * 4,
        compiler_params=params(),
        cost_estimate=cost(4 << 20, 4 << 20),
        name="grad_conv",
    )(sends_x, sums, norm, gain, conv_out, ga, mask)


def column(row):
    return jnp.transpose(jnp.broadcast_to(row, (CH, CH)))


def combine_kernel(sum_ref, norm_ref, gain_ref, w_ref, out_ref):
    totals = jnp.sum(sum_ref[...], axis=0)
    inverse, count = norm_ref[1:2], norm_ref[2:3]
    factor = column(gain_ref[...] * inverse * lax.rsqrt(count))
    first = column(totals[0:1] / count)
    second = column(totals[1:2] / count)
    for p in range(3):
        for k in range(9):
            lanes = slice(k * CH, (k + 1) * CH)
            base = w_ref[p, 0:CH, lanes]
            cross = w_ref[p, CH : 2 * CH, lanes]
            ones = w_ref[p, 2 * CH : 2 * CH + 8, lanes][0:1]
            value = factor * (base - first * ones - second * cross)
            value = value.astype(BF16)
            for g in range(8):
                out_ref[g, 9 * p + k] = value[16 * g : 16 * (g + 1)]


def combine(sums, norm, gain, terms):
    return pl.pallas_call(
        combine_kernel,
        out_shape=shape((8, 27, 16, CH), BF16),
        in_specs=[VM] * 4,
        out_specs=VM,
        compiler_params=params(),
        cost_estimate=cost(4 << 20, 5 << 20),
        name="combine",
    )(sums, norm, gain, terms)


def finish_kernel(parts_ref, out_ref):
    for t in range(27):
        rows = jnp.concatenate([parts_ref[g, t].astype(F32) for g in range(8)], axis=0)
        out_ref[t] = jnp.transpose(rows)


def finish(parts):
    return pl.pallas_call(
        finish_kernel,
        out_shape=shape((27, CH, CH), F32),
        in_specs=[VM],
        out_specs=VM,
        compiler_params=params(),
        cost_estimate=cost(1 << 20, 3 << 20),
        name="finish",
    )(parts)


def spread(value, axis):
    size = lax.axis_size(axis)
    return lax.all_to_all(jnp.broadcast_to(value[None], (size,) + value.shape), axis, 0, 0)


def all_sum_parts(value):
    return spread(jnp.sum(spread(value, "gy"), axis=0), "gx")


def reduce_weight(local):
    parts = lax.all_to_all(local, "gx", 0, 0)
    mine = jnp.sum(parts.astype(F32), axis=0).astype(BF16)
    size = lax.axis_size("gy")
    mine = jnp.concatenate((mine, jnp.zeros((size - 27, 16, CH), BF16)), axis=0)
    parts = lax.all_to_all(mine, "gy", 0, 0)
    done = jnp.sum(parts.astype(F32), axis=0).astype(BF16)
    return spread(spread(done, "gy")[:27], "gx")


def shards(
    features,
    occupancy,
    counts,
    kernel_map,
    x_send,
    y_send,
    weight,
    norm_gain,
    norm_shift,
    cotangent,
):
    row_map, sends_x, sends_y = kernel_map[0, 0], x_send[0, 0], y_send[0, 0]
    gain, shift = norm_gain.reshape(1, CH), norm_shift.reshape(1, CH)
    own, mask, low, high = prepare(counts, sends_x, features[0, 0], occupancy[0, 0])
    xl, xu = neighbours(low, high, "gx")
    low, high = pick_y(sends_y, own, xl, xu)
    yl, yu = neighbours(low, high, "gy")
    conv_out, x9, stats = conv(
        row_map, own, xl, xu, yl, yu, weight.reshape(3, 9 * CH, CH), mask, True
    )
    stats = all_sum_parts(stats)
    activations, ga, g, sums, norm = act(stats, conv_out, cotangent[0, 0], mask, gain, shift)
    sums = all_sum_parts(sums)
    terms = wgrad(g, x9)
    local = combine(sums, norm, gain, terms)
    grads, low, high, totals = grad(sends_x, sums, norm, gain, conv_out, ga, mask)
    weight_grad = finish(reduce_weight(local))
    xl, xu = neighbours(low, high, "gx")
    low, high = pick_y(sends_y, grads, xl, xu)
    yl, yu = neighbours(low, high, "gy")
    turned = jnp.transpose(weight[::-1], (0, 2, 1)).reshape(3, 9 * CH, CH)
    features_grad = conv(row_map, grads, xl, xu, yl, yu, turned, mask, False)
    scale = lax.rsqrt(norm[2])
    return (
        activations[None, None],
        features_grad[None, None],
        weight_grad,
        totals[1] * scale,
        totals[0] * scale,
    )


def solution(mesh):
    tiles = P("gx", "gy", None, None, None)
    lists = P("gx", "gy", None, None)
    return jax.shard_map(
        shards,
        mesh=mesh,
        in_specs=(tiles, lists, P("gx", "gy"), lists, lists, lists, P(), P(), P(), tiles),
        out_specs=(tiles, tiles, P(), P(), P()),
        check_vma=False,
    )
```

time: 679 us -> 209 us (0.31)
  the two profiles are of different devices: /device:TPU:1 before, /device:TPU:121 now
where the time goes in v1:
time: 209 us; the launch traced here: 208 us
  blocking collectives  69.2 us (33%)
  starting transfers between devices  48.2 us (23%)
  Pallas kernels  47.9 us (23%)
  waiting for transfers between devices  31 us (15%)
  local copies, waits for them, and re-layouts  9.16 us (4%)
    all_to_all x3, blocking collectives, spread(): lax.all_to_all(jnp.broadcast_to(value[None], (size,) + value.shape), axis...  35.6 us
    ppermute x8, waiting for transfers between devices, neighbours(): return (lax.ppermute(high, axis, up), lax.ppermute(low, axis, down))  31 us
    ppermute x8, starting transfers between devices, neighbours(): return (lax.ppermute(high, axis, up), lax.ppermute(low, axis, down))  29.5 us
    all_to_all x1, blocking collectives, reduce_weight(): parts = lax.all_to_all(local, 'gx', 0, 0)  18.7 us
    all_to_all x3, starting transfers between devices, spread(): lax.all_to_all(jnp.broadcast_to(value[None], (size,) + value.shape), axis...  18.7 us
    pallas_call x2, Pallas kernels, conv(): pl.pallas_call(functools.partial(conv_kernel, forward=forward), grid=(SLO...  15.3 us
    all_to_all x1, blocking collectives, reduce_weight(): parts = lax.all_to_all(mine, 'gy', 0, 0)  14.9 us
    pallas_call x1, Pallas kernels, wgrad(): pl.pallas_call(wgrad_kernel, grid=(SLOTS,), out_shape=shape((3, 2 * CH +...  11.6 us
  transfers between devices with their start and end apart: 11, of which 7 were waited for; matrix products, arithmetic and copies ran while one was open for 2% of the time, Pallas kernels for 12%

profile of v1, /device:TPU:121, one launch (start us, length us, event | category | flops | bytes accessed | tf_op | source)
XLA Modules:
  0.0 208.4 jit_solution(2566746481223903025)
XLA Ops:
  1.3 2.5 %prepare.1 = (bf16[4,512,128]{2,1,0:T(8,128)(2,1)}, bf16[4,512,128]{2,1,0:T(8,128)(2,1)}, bf16[2,512,128]{2,1,0:T(8,128)(2,1)}, bf16[2,512,128]{2,1,0:T(8,128)(2,1)}) custom-call(s32[1,1]{1,0:T(1,128)S(6)} %copy.17.counts_ref, s32[2,2]{1,0:T(2,128)} %bitcast.26, bf16[4,512,128]{2,1,0:T(8,128)(2,1)} %bitcast.20, s32[4,512]{1,0:T(4,128)} %bitcast.22), custom_call_target="tpu_custom_call" | custom-call | flops 1048576 | bytes 2097152 | tf_op jit(solution)/shard_map/prepare/pallas_call | solution.py:59
  3.8 4.3 %collective-permute-start = (bf16[2,512,128]{2,1,0:T(8,128)(2,1)}, bf16[2,512,128]{2,1,0:T(8,128)(2,1)S(1)}, u32[]{:S(2)}, u32[]{:S(2)}) collective-permute-start(bf16[2,512,128]{2,1,0:T(8,128)(2,1)} %get-tuple-element.26), channel_id=1, source_target_pairs={{0,32},{32,64},{64,96},{96,128},{128,160},{160,192},{192,224},{1,3... | collective-permute-start | bytes 786440 | tf_op jit(solution)/shard_map/ppermute | solution.py:113
  8.1 1.9 collective-permute-start.1
  10.0 3.3 %collective-permute-done.xl_ref = bf16[2,512,128]{2,1,0:T(8,128)(2,1)S(1)} collective-permute-done((bf16[2,512,128]{2,1,0:T(8,128)(2,1)}, bf16[2,512,128]{2,1,0:T(8,128)(2,1)S(1)}, u32[]{:S(2)}, u32[]{:S(2)}) %collective-permute-start) | collective-permute-done | bytes 262176 | tf_op jit(solution)/shard_map/ppermute | solution.py:113
  13.4 7.3 %collective-permute-done.1.xu_ref = bf16[2,512,128]{2,1,0:T(8,128)(2,1)S(1)} collective-permute-done((bf16[2,512,128]{2,1,0:T(8,128)(2,1)}, bf16[2,512,128]{2,1,0:T(8,128)(2,1)S(1)}, u32[]{:S(2)}, u32[]{:S(2)}) %collective-permute-start.1) | collective-permute-done | bytes 262176 | tf_op jit(solution)/shard_map/ppermute | solution.py:113
  20.7 0.7 copy-done.6
  21.4 2.4 %pick_y.2 = (bf16[4,512,128]{2,1,0:T(8,128)(2,1)}, bf16[4,512,128]{2,1,0:T(8,128)(2,1)}) custom-call(s32[2,4]{1,0:T(2,128)} %bitcast.28, bf16[4,512,128]{2,1,0:T(8,128)(2,1)} %get-tuple-element.25.own_ref, bf16[2,512,128]{2,1,0:T(8,128)(2,1)} %copy-done.5, bf16[2,512,128]{2,1,0:T(8,128)(2,1)} %copy-done.6), custom_call_target="tpu_custom_call" | custom-call | flops 1048576 | bytes 2097152 | tf_op jit(solution)/shard_map/pick_y/pallas_call | solution.py:98
  23.8 6.5 %collective-permute-start.2 = (bf16[4,512,128]{2,1,0:T(8,128)(2,1)}, bf16[4,512,128]{2,1,0:T(8,128)(2,1)S(1)}, u32[]{:S(2)}, u32[]{:S(2)}) collective-permute-start(bf16[4,512,128]{2,1,0:T(8,128)(2,1)} %get-tuple-element.28), channel_id=1, source_target_pairs={{0,1},{1,2},{2,3},{3,4},{4,5},{5,6},{6,7},{7,8},{8,9},{9,10},{10,1... | collective-permute-start | bytes 1572872 | tf_op jit(solution)/shard_map/ppermute | solution.py:113
  30.3 1.9 collective-permute-start.3
  32.2 4.5 %collective-permute-done.2.yl_ref = bf16[4,512,128]{2,1,0:T(8,128)(2,1)S(1)} collective-permute-done((bf16[4,512,128]{2,1,0:T(8,128)(2,1)}, bf16[4,512,128]{2,1,0:T(8,128)(2,1)S(1)}, u32[]{:S(2)}, u32[]{:S(2)}) %collective-permute-start.2) | collective-permute-done | bytes 524320 | tf_op jit(solution)/shard_map/ppermute | solution.py:113
  36.7 5.5 %collective-permute-done.3.yu_ref = bf16[4,512,128]{2,1,0:T(8,128)(2,1)S(1)} collective-permute-done((bf16[4,512,128]{2,1,0:T(8,128)(2,1)}, bf16[4,512,128]{2,1,0:T(8,128)(2,1)S(1)}, u32[]{:S(2)}, u32[]{:S(2)}) %collective-permute-start.3) | collective-permute-done | bytes 524320 | tf_op jit(solution)/shard_map/ppermute | solution.py:113
  42.2 0.8 copy-done.9
  43.0 7.9 %forward_conv.1 = (f32[4,512,128]{2,1,0:T(8,128)}, bf16[4,640,1152]{2,1,0:T(8,128)(2,1)}, f32[8,128]{1,0:T(8,128)}) custom-call(s32[4,27]{1,0:T(4,128)} %bitcast.32, bf16[4,512,128]{2,1,0:T(8,128)(2,1)} %get-tuple-element.25.own_ref, bf16[2,512,128]{2,1,0:T(8,128)(2,1)} %copy-done.5, bf16[2,512,128]{2,1,0:T(8,128)(2,1)} %copy-done.6, ...), custom_call_target="tpu_custom_call" | custom-call | flops 1811939328 | bytes 12582912 | tf_op jit(solution)/shard_map/forward_conv/pallas_call | solution.py:189
  50.9 0.7 broadcast_in_dim.16
  51.6 12.1 %all_to_all.40 = f32[32,8,128]{2,1,0:T(8,128)S(1)} all-to-all(f32[32,8,128]{2,1,0:T(8,128)S(1)} %broadcast_in_dim.16), channel_id=1, replica_groups=mesh['gx'=8,'gy'=32] {'gy'}, dimensions={0} | all-to-all | bytes 262144 | tf_op jit(solution)/shard_map/all_to_all | solution.py:386
  63.7 8.7 %all_to_all.41.stat_ref = f32[8,8,128]{2,1,0:T(8,128)} all-to-all(f32[8,8,128]{2,1,0:T(8,128)S(1)} %broadcast_in_dim.17), channel_id=1, replica_groups=mesh['gx'=8,'gy'=32] {'gx'}, dimensions={0} | all-to-all | bytes 65536 | tf_op jit(solution)/shard_map/all_to_all | solution.py:386
  72.4 4.2 %activation.1 = (bf16[4,512,128]{2,1,0:T(8,128)(2,1)}, f32[4,512,128]{2,1,0:T(8,128)}, bf16[4,272,512]{2,1,0:T(8,128)(2,1)}, f32[8,128]{1,0:T(8,128)}, f32[8,128]{1,0:T(8,128)}) custom-call(f32[8,8,128]{2,1,0:T(8,128)} %all_to_all.41.stat_ref, f32[4,512,128]{2,1,0:T(8,128)} %get-tuple-element.32.conv_ref, bf16[4,512,128]{2,1,0:T(8,128)(2,1)} %bitcast.21, ...), custom_call_target="tpu_custom_call" | custom-call | flops 8388608 | bytes 5242880 | tf_op jit(solution)/shard_map/activation/pallas_call | solution.py:247
  76.6 0.7 broadcast_in_dim.19
  77.3 14.9 %all_to_all.42 = f32[32,8,128]{2,1,0:T(8,128)S(1)} all-to-all(f32[32,8,128]{2,1,0:T(8,128)S(1)} %broadcast_in_dim.19), channel_id=1, replica_groups=mesh['gx'=8,'gy'=32] {'gy'}, dimensions={0} | all-to-all | bytes 262144 | tf_op jit(solution)/shard_map/all_to_all | solution.py:386
  92.2 0.6 broadcast_in_dim.20
  92.8 5.0 %all-to-all-start.3 = ((f32[8,8,128]{2,1,0:T(8,128)}), f32[8,8,128]{2,1,0:T(8,128)S(1)}, u32[]{:S(2)}, u32[]{:S(2)}) async-start(f32[8,8,128]{2,1,0:T(8,128)} %broadcast_in_dim.20), calls=%async_computation.3 | async-start | bytes 65536 | tf_op jit(solution)/shard_map/all_to_all | solution.py:386
  97.9 11.6 %weight_terms.1.w_ref = f32[3,272,1152]{2,1,0:T(8,128)} custom-call(bf16[4,272,512]{2,1,0:T(8,128)(2,1)} %get-tuple-element.42.g_ref, bf16[4,640,1152]{2,1,0:T(8,128)(2,1)} %get-tuple-element.43.x9_ref), custom_call_target="tpu_custom_call" | custom-call | flops 3623878656 | bytes 12582912 | tf_op jit(solution)/shard_map/weight_terms/pallas_call | solution.py:288
  109.4 0.6 copy-done.2
  110.0 3.5 %combine.1 = bf16[8,27,16,128]{3,2,1,0:T(8,128)(2,1)} custom-call(f32[8,8,128]{2,1,0:T(8,128)} %copy-done.2, f32[8,128]{1,0:T(8,128)} %get-tuple-element.35.norm_ref, f32[1,128]{1,0:T(1,128)} %bitcast.24, f32[3,272,1152]{2,1,0:T(8,128)} %weight_terms.1.w_ref), custom_call_target="tpu_custom_call" | custom-call | flops 4194304 | bytes 5242880 | tf_op jit(solution)/shard_map/combine/pallas_call | solution.py:355
  113.5 18.7 %all_to_all.43 = bf16[8,27,16,128]{3,2,1,0:T(8,128)(2,1)S(1)} all-to-all(bf16[8,27,16,128]{3,2,1,0:T(8,128)(2,1)} %combine.1), channel_id=1, replica_groups=mesh['gx'=8,'gy'=32] {'gx'}, dimensions={0} | all-to-all | bytes 1769472 | tf_op jit(solution)/shard_map/all_to_all | solution.py:394
  132.2 0.1 reduce_sum.44
  132.4 0.0 copy-start.1
  132.4 14.9 %all_to_all.44 = bf16[32,16,128]{2,1,0:T(8,128)(2,1)S(1)} all-to-all(bf16[32,16,128]{2,1,0:T(8,128)(2,1)S(1)} %concatenate.3), channel_id=1, replica_groups=mesh['gx'=8,'gy'=32] {'gy'}, dimensions={0} | all-to-all | bytes 262144 | tf_op jit(solution)/shard_map/all_to_all | solution.py:398
  147.3 0.7 broadcast_in_dim.22
  148.0 7.0 %all-to-all-start.6 = ((bf16[32,16,128]{2,1,0:T(8,128)(2,1)}), bf16[32,16,128]{2,1,0:T(8,128)(2,1)S(1)}, u32[]{:S(2)}, u32[]{:S(2)}) async-start(bf16[32,16,128]{2,1,0:T(8,128)(2,1)} %broadcast_in_dim.22), calls=%async_computation.6 | async-start | bytes 262144 | tf_op jit(solution)/shard_map/all_to_all | solution.py:386
  155.0 3.2 %grad_conv.1 = (bf16[4,512,128]{2,1,0:T(8,128)(2,1)}, bf16[2,512,128]{2,1,0:T(8,128)(2,1)}, bf16[2,512,128]{2,1,0:T(8,128)(2,1)}, f32[8,128]{1,0:T(8,128)}) custom-call(s32[2,2]{1,0:T(2,128)} %bitcast.27, f32[8,8,128]{2,1,0:T(8,128)} %copy-done.2, f32[8,128]{1,0:T(8,128)} %get-tuple-element.35.norm_ref, f32[1,128]{1,0:T(1,128)} %bitcast.25, ...), custom_call_target="tpu_custom_call" | custom-call | flops 4194304 | bytes 4194304 | tf_op jit(solution)/shard_map/grad_conv/pallas_call | solution.py:316
  158.2 4.3 %collective-permute-start.4 = (bf16[2,512,128]{2,1,0:T(8,128)(2,1)}, bf16[2,512,128]{2,1,0:T(8,128)(2,1)S(1)}, u32[]{:S(2)}, u32[]{:S(2)}) collective-permute-start(bf16[2,512,128]{2,1,0:T(8,128)(2,1)} %get-tuple-element.38), channel_id=1, source_target_pairs={{0,32},{32,64},{64,96},{96,128},{128,160},{160,192},{192,224},{1,3... | collective-permute-start | bytes 786440 | tf_op jit(solution)/shard_map/ppermute | solution.py:113
  162.5 1.9 collective-permute-start.5
  164.5 1.0 broadcast_in_dim.23
  165.5 6.6 %all-to-all-start.7 = ((bf16[8,27,16,128]{3,2,1,0:T(8,128)(2,1)}), bf16[8,27,16,128]{3,2,1,0:T(8,128)(2,1)S(1)}, u32[]{:S(2)}, u32[]{:S(2)}) async-start(bf16[8,27,16,128]{3,2,1,0:T(8,128)(2,1)} %broadcast_in_dim.23), calls=%async_computation.7 | async-start | bytes 1769472 | tf_op jit(solution)/shard_map/all_to_all | solution.py:386
  172.1 3.3 %collective-permute-done.5.xu_ref = bf16[2,512,128]{2,1,0:T(8,128)(2,1)S(1)} collective-permute-done((bf16[2,512,128]{2,1,0:T(8,128)(2,1)}, bf16[2,512,128]{2,1,0:T(8,128)(2,1)S(1)}, u32[]{:S(2)}, u32[]{:S(2)}) %collective-permute-start.5) | collective-permute-done | bytes 262176 | tf_op jit(solution)/shard_map/ppermute | solution.py:113
  175.4 0.7 copy-done.4
  176.1 2.4 %pick_y.3 = (bf16[4,512,128]{2,1,0:T(8,128)(2,1)}, bf16[4,512,128]{2,1,0:T(8,128)(2,1)}) custom-call(s32[2,4]{1,0:T(2,128)} %bitcast.29, bf16[4,512,128]{2,1,0:T(8,128)(2,1)} %get-tuple-element.37.own_ref, bf16[2,512,128]{2,1,0:T(8,128)(2,1)} %copy-done.3, bf16[2,512,128]{2,1,0:T(8,128)(2,1)} %copy-done.4), custom_call_target="tpu_custom_call" | custom-call | flops 1048576 | bytes 2097152 | tf_op jit(solution)/shard_map/pick_y/pallas_call | solution.py:98
  178.6 6.8 %collective-permute-start.6 = (bf16[4,512,128]{2,1,0:T(8,128)(2,1)}, bf16[4,512,128]{2,1,0:T(8,128)(2,1)S(1)}, u32[]{:S(2)}, u32[]{:S(2)}) collective-permute-start(bf16[4,512,128]{2,1,0:T(8,128)(2,1)} %get-tuple-element.40), channel_id=1, source_target_pairs={{0,1},{1,2},{2,3},{3,4},{4,5},{5,6},{6,7},{7,8},{8,9},{9,10},{10,1... | collective-permute-start | bytes 1572872 | tf_op jit(solution)/shard_map/ppermute | solution.py:113
  185.3 1.9 collective-permute-start.7
  187.3 0.1 reverse_bitcast_fusion
  187.4 1.6 copy.16
  189.0 1.3 multiply_bitcast_fusion
  190.3 1.5 collective-permute-done.6.yl_ref
  191.8 5.6 %collective-permute-done.7.yu_ref = bf16[4,512,128]{2,1,0:T(8,128)(2,1)} collective-permute-done((bf16[4,512,128]{2,1,0:T(8,128)(2,1)}, bf16[4,512,128]{2,1,0:T(8,128)(2,1)}, u32[]{:S(2)}, u32[]{:S(2)}) %collective-permute-start.7) | collective-permute-done | bytes 524320 | tf_op jit(solution)/shard_map/ppermute | solution.py:113
  197.4 7.4 %transposed_conv.1 = bf16[4,512,128]{2,1,0:T(8,128)(2,1)} custom-call(s32[4,27]{1,0:T(4,128)} %bitcast.33, bf16[4,512,128]{2,1,0:T(8,128)(2,1)} %get-tuple-element.37.own_ref, bf16[2,512,128]{2,1,0:T(8,128)(2,1)} %copy-done.3, bf16[2,512,128]{2,1,0:T(8,128)(2,1)} %copy-done.4, bf16[4,512,128]{2,1,0:T(8,128)(2,1)} %copy-done.7, ...), custom_call_target="tpu_custom_call" | custom-call | flops 1811939328 | bytes 12582912 | tf_op jit(solution)/shard_map/transposed_conv/pallas_call | solution.py:189
  204.8 0.9 copy-done
  205.7 2.7 %finish.1 = f32[27,128,128]{2,1,0:T(8,128)} custom-call(bf16[8,27,16,128]{3,2,1,0:T(8,128)(2,1)} %copy-done), custom_call_target="tpu_custom_call" | custom-call | flops 1048576 | bytes 3145728 | tf_op jit(solution)/shard_map/finish/pallas_call | solution.py:373
  (24 shorter events, 0.2 us)
Async XLA Ops:
  3.8 9.6 %collective-permute-start = (bf16[2,512,128]{2,1,0:T(8,128)(2,1)}, bf16[2,512,128]{2,1,0:T(8,128)(2,1)S(1)}, u32[]{:S(2)}, u32[]{:S(2)}) collective-permute-start(bf16[2,512,128]{2,1,0:T(8,128)(2,1)} %get-tuple-element.26), channel_id=1, source_target_pairs={{0,32},{32,64},{64,96},{96,128},{128,160},{160,192},{192,224},{1,3... | collective-permute-start | bytes 786440 | tf_op jit(solution)/shard_map/ppermute | solution.py:113
  8.1 12.6 %collective-permute-start.1 = (bf16[2,512,128]{2,1,0:T(8,128)(2,1)}, bf16[2,512,128]{2,1,0:T(8,128)(2,1)S(1)}, u32[]{:S(2)}, u32[]{:S(2)}) collective-permute-start(bf16[2,512,128]{2,1,0:T(8,128)(2,1)} %get-tuple-element.27), channel_id=1, source_target_pairs={{32,0},{64,32},{96,64},{128,96},{160,128},{192,160},{224,192},{33,... | collective-permute-start | bytes 786440 | tf_op jit(solution)/shard_map/ppermute | solution.py:113
  13.4 7.3 %copy-start.5 = (bf16[2,512,128]{2,1,0:T(8,128)(2,1)}, bf16[2,512,128]{2,1,0:T(8,128)(2,1)S(1)}, u32[]{:S(2)}) copy-start(bf16[2,512,128]{2,1,0:T(8,128)(2,1)S(1)} %collective-permute-done.xl_ref) | copy-start | bytes 786436
  20.7 0.7 copy-start.6
  23.8 12.9 %collective-permute-start.2 = (bf16[4,512,128]{2,1,0:T(8,128)(2,1)}, bf16[4,512,128]{2,1,0:T(8,128)(2,1)S(1)}, u32[]{:S(2)}, u32[]{:S(2)}) collective-permute-start(bf16[4,512,128]{2,1,0:T(8,128)(2,1)} %get-tuple-element.28), channel_id=1, source_target_pairs={{0,1},{1,2},{2,3},{3,4},{4,5},{5,6},{6,7},{7,8},{8,9},{9,10},{10,1... | collective-permute-start | bytes 1572872 | tf_op jit(solution)/shard_map/ppermute | solution.py:113
  30.3 11.9 %collective-permute-start.3 = (bf16[4,512,128]{2,1,0:T(8,128)(2,1)}, bf16[4,512,128]{2,1,0:T(8,128)(2,1)S(1)}, u32[]{:S(2)}, u32[]{:S(2)}) collective-permute-start(bf16[4,512,128]{2,1,0:T(8,128)(2,1)} %get-tuple-element.29), channel_id=1, source_target_pairs={{1,0},{2,1},{3,2},{4,3},{5,4},{6,5},{7,6},{8,7},{9,8},{10,9},{11,1... | collective-permute-start | bytes 1572872 | tf_op jit(solution)/shard_map/ppermute | solution.py:113
  36.7 5.5 %copy-start.8 = (bf16[4,512,128]{2,1,0:T(8,128)(2,1)}, bf16[4,512,128]{2,1,0:T(8,128)(2,1)S(1)}, u32[]{:S(2)}) copy-start(bf16[4,512,128]{2,1,0:T(8,128)(2,1)S(1)} %collective-permute-done.2.yl_ref) | copy-start | bytes 1572868
  42.2 0.8 copy-start.9
  92.8 16.6 %all-to-all-start.3 = ((f32[8,8,128]{2,1,0:T(8,128)}), f32[8,8,128]{2,1,0:T(8,128)S(1)}, u32[]{:S(2)}, u32[]{:S(2)}) async-start(f32[8,8,128]{2,1,0:T(8,128)} %broadcast_in_dim.20), calls=%async_computation.3 | async-start | bytes 65536 | tf_op jit(solution)/shard_map/all_to_all | solution.py:386
  109.4 0.6 copy-start.2
  132.4 54.9 %copy-start.1 = (bf16[27,128,128]{2,1,0:T(8,128)(2,1)S(1)}, bf16[27,128,128]{2,1,0:T(8,128)(2,1)}, u32[]{:S(2)}) copy-start(bf16[27,128,128]{2,1,0:T(8,128)(2,1)} %param.16) | copy-start | bytes 2654212
  148.0 16.4 %all-to-all-start.6 = ((bf16[32,16,128]{2,1,0:T(8,128)(2,1)}), bf16[32,16,128]{2,1,0:T(8,128)(2,1)S(1)}, u32[]{:S(2)}, u32[]{:S(2)}) async-start(bf16[32,16,128]{2,1,0:T(8,128)(2,1)} %broadcast_in_dim.22), calls=%async_computation.6 | async-start | bytes 262144 | tf_op jit(solution)/shard_map/all_to_all | solution.py:386
  158.2 13.9 %collective-permute-start.4 = (bf16[2,512,128]{2,1,0:T(8,128)(2,1)}, bf16[2,512,128]{2,1,0:T(8,128)(2,1)S(1)}, u32[]{:S(2)}, u32[]{:S(2)}) collective-permute-start(bf16[2,512,128]{2,1,0:T(8,128)(2,1)} %get-tuple-element.38), channel_id=1, source_target_pairs={{0,32},{32,64},{64,96},{96,128},{128,160},{160,192},{192,224},{1,3... | collective-permute-start | bytes 786440 | tf_op jit(solution)/shard_map/ppermute | solution.py:113
  162.5 12.9 %collective-permute-start.5 = (bf16[2,512,128]{2,1,0:T(8,128)(2,1)}, bf16[2,512,128]{2,1,0:T(8,128)(2,1)S(1)}, u32[]{:S(2)}, u32[]{:S(2)}) collective-permute-start(bf16[2,512,128]{2,1,0:T(8,128)(2,1)} %get-tuple-element.39), channel_id=1, source_target_pairs={{32,0},{64,32},{96,64},{128,96},{160,128},{192,160},{224,192},{33,... | collective-permute-start | bytes 786440 | tf_op jit(solution)/shard_map/ppermute | solution.py:113
  165.5 39.3 %all-to-all-start.7 = ((bf16[8,27,16,128]{3,2,1,0:T(8,128)(2,1)}), bf16[8,27,16,128]{3,2,1,0:T(8,128)(2,1)S(1)}, u32[]{:S(2)}, u32[]{:S(2)}) async-start(bf16[8,27,16,128]{3,2,1,0:T(8,128)(2,1)} %broadcast_in_dim.23), calls=%async_computation.7 | async-start | bytes 1769472 | tf_op jit(solution)/shard_map/all_to_all | solution.py:386
  172.1 3.3 %copy-start.3 = (bf16[2,512,128]{2,1,0:T(8,128)(2,1)}, bf16[2,512,128]{2,1,0:T(8,128)(2,1)S(1)}, u32[]{:S(2)}) copy-start(bf16[2,512,128]{2,1,0:T(8,128)(2,1)S(1)} %collective-permute-done.4.xl_ref) | copy-start | bytes 786436
  175.4 0.7 copy-start.4
  178.6 13.2 %collective-permute-start.6 = (bf16[4,512,128]{2,1,0:T(8,128)(2,1)}, bf16[4,512,128]{2,1,0:T(8,128)(2,1)S(1)}, u32[]{:S(2)}, u32[]{:S(2)}) collective-permute-start(bf16[4,512,128]{2,1,0:T(8,128)(2,1)} %get-tuple-element.40), channel_id=1, source_target_pairs={{0,1},{1,2},{2,3},{3,4},{4,5},{5,6},{6,7},{7,8},{8,9},{9,10},{10,1... | collective-permute-start | bytes 1572872 | tf_op jit(solution)/shard_map/ppermute | solution.py:113
  185.3 12.0 %collective-permute-start.7 = (bf16[4,512,128]{2,1,0:T(8,128)(2,1)}, bf16[4,512,128]{2,1,0:T(8,128)(2,1)}, u32[]{:S(2)}, u32[]{:S(2)}) collective-permute-start(bf16[4,512,128]{2,1,0:T(8,128)(2,1)} %get-tuple-element.41), channel_id=1, source_target_pairs={{1,0},{2,1},{3,2},{4,3},{5,4},{6,5},{7,6},{8,7},{9,8},{10,9},{11,1... | collective-permute-start | bytes 1572872 | tf_op jit(solution)/shard_map/ppermute | solution.py:113
  191.8 5.6 %copy-start.7 = (bf16[4,512,128]{2,1,0:T(8,128)(2,1)}, bf16[4,512,128]{2,1,0:T(8,128)(2,1)S(1)}, u32[]{:S(2)}) copy-start(bf16[4,512,128]{2,1,0:T(8,128)(2,1)S(1)} %collective-permute-done.6.yl_ref) | copy-start | bytes 1572868
  204.8 0.9 copy-start

commit v2 on v1

v2 whole, which is shorter than its diff:
```python
import functools

import jax
import jax.numpy as jnp
from jax import lax
from jax.experimental import pallas as pl
from jax.experimental.pallas import tpu as pltpu
from jax.sharding import PartitionSpec as P

EDGE = 8
PLANE = 64
VOX = 512
CH = 128
SLOTS = 4
HX = 2
HY = 4
EPSILON = 1e-05
F32 = jnp.float32
BF16 = jnp.bfloat16

VM = pl.BlockSpec(memory_space=pltpu.VMEM)
SM = pl.BlockSpec(memory_space=pltpu.SMEM)
MAIN = 224
EXTRA = 48
FACE_ROWS = HY * PLANE + 16
MIB = 1024 * 1024
CROSS = ("xh", "y", "xl")


def params(limit=20):
    return pltpu.CompilerParams(vmem_limit_bytes=limit * MIB)


def cost(flops, moved):
    return pl.CostEstimate(flops=flops, bytes_accessed=moved, transcendentals=0)


def shape(dims, kind):
    return jax.ShapeDtypeStruct(dims, kind)


def pick_x(sends_ref, own_ref, low_ref, high_ref, faces):
    for side, out_ref in ((0, low_ref), (1, high_ref)):
        start, stop = (0, VOX) if not faces else ((0, PLANE), (VOX - PLANE, VOX))[side]
        for k in range(HX):
            row = sends_ref[side, k]
            brick = own_ref[jnp.minimum(row, SLOTS - 1), start:stop, :]
            out_ref[k] = jnp.where(row < SLOTS, brick, jnp.zeros_like(brick))


def x_shapes(faces):
    send = shape((HX, PLANE if faces else VOX, CH), BF16)
    return (send, send)


def prepare_kernel(
    counts_ref, sends_ref, feat_ref, occ_ref, own_ref, mask_ref, low_ref, high_ref, *, faces
):
    for s in range(SLOTS):
        live = (s < counts_ref[0, 0]).astype(F32)
        for k in range(VOX // CH):
            row = occ_ref[s : s + 1, k * CH : (k + 1) * CH].astype(F32) * live
            column = jnp.transpose(jnp.broadcast_to(row, (CH, CH)))
            rows = pl.ds(k * CH, CH)
            mask_ref[s, rows, :] = column.astype(BF16)
            own_ref[s, rows, :] = (feat_ref[s, rows, :].astype(F32) * column).astype(BF16)
    pick_x(sends_ref, own_ref, low_ref, high_ref, faces)


def prepare(counts, sends_x, features, occupancy, faces):
    return pl.pallas_call(
        functools.partial(prepare_kernel, faces=faces),
        out_shape=(shape((SLOTS, VOX, CH), BF16),) * 2 + x_shapes(faces),
        in_specs=[SM, SM, VM, VM],
        out_specs=(VM, VM, VM, VM),
        compiler_params=params(),
        cost_estimate=cost(1 << 20, 2 << 20),
        name="prepare",
    )(counts, sends_x, features, occupancy)


def pick_y_kernel(sends_ref, own_ref, xl_ref, xu_ref, low_ref, high_ref):
    for side, out_ref in ((0, low_ref), (1, high_ref)):
        for k in range(HY):
            row = sends_ref[side, k]

            @pl.when(row < SLOTS)
            def _():
                out_ref[k] = own_ref[jnp.minimum(row, SLOTS - 1)]

            @pl.when((row >= SLOTS) & (row < SLOTS + HX))
            def _():
                out_ref[k] = xl_ref[jnp.clip(row - SLOTS, 0, HX - 1)]

            @pl.when((row >= SLOTS + HX) & (row < SLOTS + 2 * HX))
            def _():
                out_ref[k] = xu_ref[jnp.clip(row - SLOTS - HX, 0, HX - 1)]

            @pl.when(row >= SLOTS + 2 * HX)
            def _():
                out_ref[k] = jnp.zeros((VOX, CH), BF16)


def pick_y_faces_kernel(sends_ref, own_ref, xl_ref, xu_ref, low_ref, high_ref):
    lines = lax.broadcasted_iota(jnp.int32, (16, CH), 0)
    for side, out_ref in ((0, low_ref), (1, high_ref)):
        skip = 0 if side == 0 else PLANE - 16

        def edge(block):
            block = block.astype(F32)
            return block[:EDGE] if side == 0 else block[EDGE:]

        origin = jnp.zeros((16, CH), F32)
        for k in range(HY):
            row = sends_ref[side, k]
            rows = pl.ds(k * PLANE, PLANE)
            lower = (row >= SLOTS) & (row < SLOTS + HX)
            upper = (row >= SLOTS + HX) & (row < SLOTS + 2 * HX)
            code = jnp.where(lower, 1.0, jnp.where(upper, 2.0, 0.0))
            origin = jnp.where(lines == k, code, origin)

            @pl.when(row < SLOTS)
            def _():
                brick = jnp.minimum(row, SLOTS - 1)
                parts = [
                    edge(own_ref[brick, a * PLANE + skip : a * PLANE + skip + 16, :])
                    for a in range(EDGE)
                ]
                out_ref[rows, :] = jnp.concatenate(parts, axis=0).astype(BF16)

            @pl.when(lower)
            def _():
                part = edge(xl_ref[jnp.clip(row - SLOTS, 0, HX - 1), skip : skip + 16, :])
                empty = jnp.zeros((PLANE - EDGE, CH), F32)
                out_ref[rows, :] = jnp.concatenate((empty, part), axis=0).astype(BF16)

            @pl.when(upper)
            def _():
                part = edge(xu_ref[jnp.clip(row - SLOTS - HX, 0, HX - 1), skip : skip + 16, :])
                empty = jnp.zeros((PLANE - EDGE, CH), F32)
                out_ref[rows, :] = jnp.concatenate((part, empty), axis=0).astype(BF16)

            @pl.when(row >= SLOTS + 2 * HX)
            def _():
                out_ref[rows, :] = jnp.zeros((PLANE, CH), BF16)

        out_ref[HY * PLANE : FACE_ROWS, :] = origin.astype(BF16)


def pick_y(sends_y, own, xl, xu, faces):
    send = shape((FACE_ROWS, CH) if faces else (HY, VOX, CH), BF16)
    return pl.pallas_call(
        pick_y_faces_kernel if faces else pick_y_kernel,
        out_shape=(send, send),
        in_specs=[SM, VM, VM, VM],
        out_specs=(VM, VM),
        compiler_params=params(),
        cost_estimate=cost(1 << 20, 2 << 20),
        name="pick_y",
    )(sends_y, own, xl, xu)


def axis_size(axes):
    size = 1
    for axis in axes:
        size *= lax.axis_size(axis)
    return size


def neighbours(low, high, axis):
    size = axis_size(axis)
    up = [(i, i + 1) for i in range(size - 1)]
    down = [(j, i) for i, j in up]
    return lax.ppermute(high, axis, up), lax.ppermute(low, axis, down)


def fill_columns(map_ref, slot, table_ref, x9_ref):
    sub = lax.broadcasted_iota(jnp.int32, (EDGE + 2, EDGE, CH), 1)
    for a in range(-1, EDGE + 1):
        move = -1 if a < 0 else (1 if a >= EDGE else 0)
        base = (a % EDGE) * PLANE
        spans = []
        for r in (-1, 0, 1):
            tap = 9 * (move + 1) + r + 1
            before = table_ref[map_ref[slot, tap], base + 48 : base + 64, :].astype(F32)[8:]
            middle = table_ref[map_ref[slot, tap + 3], base : base + 64, :].astype(F32)
            after = table_ref[map_ref[slot, tap + 6], base : base + 16, :].astype(F32)[:8]
            spans.append(jnp.concatenate((before, middle, after), axis=0).reshape(EDGE + 2, EDGE, CH))
        low, centre, high = spans
        down = pltpu.roll(jnp.where(sub == EDGE - 1, low, centre), 1, 1)
        up = pltpu.roll(jnp.where(sub == 0, high, centre), EDGE - 1, 1)
        for r, source in ((-1, down), (0, centre), (1, up)):
            for q in (-1, 0, 1):
                rows = source[q + 1 : q + 1 + EDGE].reshape(PLANE, CH).astype(BF16)
                lane = (3 * (q + 1) + r + 1) * CH
                x9_ref[(a + 1) * PLANE : (a + 2) * PLANE, lane : lane + CH] = rows


def fill_whole(table_ref, refs):
    start = 0
    for ref in refs:
        table_ref[start : start + ref.shape[0]] = ref[...]
        start += ref.shape[0]


def fill_faces(table_ref, refs):
    own_ref, xl_ref, xu_ref, yl_ref, yu_ref = refs
    table_ref[0:SLOTS] = own_ref[...]
    for k in range(HX):
        table_ref[SLOTS + k, VOX - PLANE : VOX, :] = xl_ref[k]
        table_ref[SLOTS + HX + k, 0:PLANE, :] = xu_ref[k]
    empty = jnp.zeros((EDGE, CH), F32)
    first = SLOTS + 2 * HX
    for k in range(HY):
        low = yl_ref[k * PLANE : (k + 1) * PLANE, :].astype(F32)
        high = yu_ref[k * PLANE : (k + 1) * PLANE, :].astype(F32)
        for a in range(EDGE):
            part = slice(a * EDGE, (a + 1) * EDGE)
            base = a * PLANE
            table_ref[first + k, base + 48 : base + 64, :] = jnp.concatenate(
                (empty, low[part]), axis=0
            ).astype(BF16)
            table_ref[first + HY + k, base : base + 16, :] = jnp.concatenate(
                (high[part], empty), axis=0
            ).astype(BF16)


def count_misfits(rows, yl_ref, yu_ref):
    lane = lax.broadcasted_iota(jnp.int32, rows.shape, 1)
    within = lane - jnp.where(lane >= 9, 9, 0) - jnp.where(lane >= 18, 9, 0)
    not_down, not_up = lane >= 9, lane < 18
    bad = (rows >= SLOTS) & (rows < SLOTS + HX) & not_down
    bad = bad | ((rows >= SLOTS + HX) & (rows < SLOTS + 2 * HX) & not_up)
    for start, ref, wrong in (
        (SLOTS + 2 * HX, yl_ref, within >= 3),
        (SLOTS + 2 * HX + HY, yu_ref, within < 6),
    ):
        origin = ref[HY * PLANE : FACE_ROWS, :].astype(F32)
        for k in range(HY):
            code = jnp.broadcast_to(origin[k : k + 1, 0 : rows.shape[1]], rows.shape)
            fault = wrong | ((code == 1.0) & not_down) | ((code == 2.0) & not_up)
            bad = bad | ((rows == start + k) & fault)
    return jnp.sum(jnp.where(bad, 1.0, 0.0))


def conv_kernel(
    map_ref, rows_ref, own_ref, xl_ref, xu_ref, yl_ref, yu_ref, w_ref, mask_ref, *rest, forward, faces
):
    slot = pl.program_id(0)
    if forward:
        out_ref, x9_out, stat_ref, table_ref = rest
        x9_ref = x9_out.at[0]
    else:
        out_ref, table_ref, x9_ref = rest

    @pl.when(slot == 0)
    def _():
        fill = fill_faces if faces else fill_whole
        fill(table_ref, (own_ref, xl_ref, xu_ref, yl_ref, yu_ref))
        table_ref[16] = jnp.zeros((VOX, CH), BF16)
        if forward:
            stat_ref[...] = jnp.zeros_like(stat_ref)
            if faces:
                stat_ref[3:4] = jnp.broadcast_to(
                    count_misfits(rows_ref[...], yl_ref, yu_ref), (1, CH)
                )

    fill_columns(map_ref, slot, table_ref, x9_ref)
    total = None
    for p in range(3):
        term = jnp.dot(
            x9_ref[p * PLANE : p * PLANE + VOX, :], w_ref[p], preferred_element_type=F32
        )
        total = term if total is None else total + term
    mask = mask_ref[0].astype(F32)
    masked = total * mask
    if forward:
        out_ref[0] = total
        stat_ref[0:1] += jnp.sum(masked, axis=0, keepdims=True)
        stat_ref[1:2] += jnp.sum(masked * total, axis=0, keepdims=True)
        stat_ref[2:3] += jnp.sum(mask, axis=0, keepdims=True)
    else:
        out_ref[0] = masked.astype(BF16)


def whole(*dims):
    return pl.BlockSpec(dims, lambda s: (0,) * len(dims))


def conv(row_map, own, xl, xu, yl, yu, weight, mask, forward, faces):
    brick = pl.BlockSpec((1, VOX, CH), lambda s: (s, 0, 0))
    scratch = [pltpu.VMEM((17, VOX, CH), BF16)]
    if forward:
        out_shape = (
            shape((SLOTS, VOX, CH), F32),
            shape((SLOTS, 10 * PLANE, 9 * CH), BF16),
            shape((8, CH), F32),
        )
        out_specs = (brick, pl.BlockSpec((1, 10 * PLANE, 9 * CH), lambda s: (s, 0, 0)), whole(8, CH))
    else:
        out_shape = shape((SLOTS, VOX, CH), BF16)
        out_specs = brick
        scratch.append(pltpu.VMEM((10 * PLANE, 9 * CH), BF16))
    return pl.pallas_call(
        functools.partial(conv_kernel, forward=forward, faces=faces),
        grid=(SLOTS,),
        out_shape=out_shape,
        in_specs=[
            SM,
            whole(*row_map.shape),
            whole(*own.shape),
            whole(*xl.shape),
            whole(*xu.shape),
            whole(*yl.shape),
            whole(*yu.shape),
            whole(3, 9 * CH, CH),
            brick,
        ],
        out_specs=out_specs,
        scratch_shapes=scratch,
        compiler_params=params(24),
        cost_estimate=cost(1811939328, 12 << 20),
        name="forward_conv" if forward else "transposed_conv",
    )(row_map, row_map, own, xl, xu, yl, yu, weight, mask)


def norm_terms(stats):
    count = stats[2:3]
    mean = stats[0:1] / count
    variance = stats[1:2] / count - mean * mean
    return count, mean, lax.rsqrt(variance + EPSILON)


def act_kernel(stat_ref, conv_ref, cot_ref, mask_ref, gain_ref, shift_ref, act_ref, ga_ref, g_ref, sum_ref, norm_ref):
    slot = pl.program_id(0)
    count, mean, inverse = norm_terms(jnp.sum(stat_ref[...], axis=0))

    @pl.when(slot == 0)
    def _():
        sum_ref[...] = jnp.zeros_like(sum_ref)
        norm_ref[...] = jnp.concatenate((mean, inverse, count, jnp.zeros((5, CH), F32)), axis=0)

    mask = mask_ref[0].astype(F32)
    normed = (conv_ref[0] - mean) * inverse
    pre = gain_ref[...] * normed + shift_ref[...]
    sig = jax.nn.sigmoid(pre)
    act_ref[0] = (pre * sig * mask).astype(BF16)
    ga = cot_ref[0].astype(F32) * mask * sig * (1.0 + pre * (1.0 - sig))
    ga_ref[0] = ga
    sum_ref[0:1] += jnp.sum(ga, axis=0, keepdims=True)
    sum_ref[1:2] += jnp.sum(ga * normed, axis=0, keepdims=True)
    nm = normed * mask
    for k in range(VOX // CH):
        rows = slice(k * CH, (k + 1) * CH)
        g_ref[0, 0:CH, rows] = jnp.transpose(ga[rows]).astype(BF16)
        g_ref[0, CH : 2 * CH, rows] = jnp.transpose(nm[rows]).astype(BF16)
        g_ref[0, 2 * CH : 2 * CH + 16, rows] = jnp.transpose(mask[rows])[0:16].astype(BF16)


def act(stats, conv_out, cotangent, mask, gain, shift):
    brick = pl.BlockSpec((1, VOX, CH), lambda s: (s, 0, 0))
    return pl.pallas_call(
        act_kernel,
        grid=(SLOTS,),
        out_shape=(
            shape((SLOTS, VOX, CH), BF16),
            shape((SLOTS, VOX, CH), F32),
            shape((SLOTS, 2 * CH + 16, VOX), BF16),
            shape((8, CH), F32),
            shape((8, CH), F32),
        ),
        in_specs=[whole(*stats.shape), brick, brick, brick, whole(1, CH), whole(1, CH)],
        out_specs=(
            brick,
            brick,
            pl.BlockSpec((1, 2 * CH + 16, VOX), lambda s: (s, 0, 0)),
            whole(8, CH),
            whole(8, CH),
        ),
        compiler_params=params(),
        cost_estimate=cost(8 << 20, 5 << 20),
        name="activation",
    )(stats, conv_out, cotangent, mask, gain, shift)


def split(value, pieces):
    parts = []
    for _ in range(pieces):
        part = value.astype(BF16).astype(F32)
        parts.append(part)
        value = value - part
    return parts


def pack(ones, sums):
    parts = split(ones, 2) + split(sums[0:1], 3) + split(sums[1:2], 3)
    used = sum(part.shape[0] for part in parts)
    rows = -(-used // 16) * 16
    if used < rows:
        parts.append(jnp.zeros((rows - used, CH), F32))
    return jnp.concatenate(parts, axis=0).astype(BF16)


def unpack(rows, taps):
    ones = rows[0:taps] + rows[taps : 2 * taps]
    at = 2 * taps
    first = rows[at : at + 1] + rows[at + 1 : at + 2] + rows[at + 2 : at + 3]
    second = rows[at + 3 : at + 4] + rows[at + 4 : at + 5] + rows[at + 5 : at + 6]
    return ones, jnp.concatenate((first, second), axis=0)


def wgrad_kernel(core_ref, g_ref, x9_ref, sum_ref, keep_ref, send_ref, full_ref):
    ones = [None] * 27
    for p in range(3):
        for q in range(3):
            lanes = slice(3 * q * CH, 3 * (q + 1) * CH)
            total = None
            for s in range(SLOTS):
                term = jnp.dot(
                    g_ref[s],
                    x9_ref[s, p * PLANE : p * PLANE + VOX, lanes],
                    preferred_element_type=F32,
                )
                total = term if total is None else total + term
            for r in range(3):
                t = 9 * p + 3 * q + r
                tap = total[:, r * CH : (r + 1) * CH]
                ones[t] = tap[2 * CH : 2 * CH + 1]
                for half in (0, 1):
                    i = t - 13 * half
                    if 0 <= i < 14:
                        for k in range(16):
                            pair = jnp.concatenate(
                                (tap[8 * k : 8 * k + 8], tap[CH + 8 * k : CH + 8 * k + 8]), axis=0
                            )
                            row = k * MAIN + i * 16
                            full_ref[half, row : row + 16, :] = pair.astype(BF16)
    for half in (0, 1):
        rows = jnp.concatenate(ones[13 * half : 13 * half + 14], axis=0)
        full_ref[half, 16 * MAIN : 16 * MAIN + EXTRA, :] = pack(rows, sum_ref[0:2])
    core = core_ref[0]
    keep_ref[...] = full_ref[core]
    send_ref[...] = full_ref[1 - core]


def wgrad(core, g, x9, sums):
    rows = 16 * MAIN + EXTRA
    return pl.pallas_call(
        wgrad_kernel,
        out_shape=(shape((rows, CH), BF16), shape((rows, CH), BF16)),
        in_specs=[SM, VM, VM, VM],
        out_specs=(VM, VM),
        scratch_shapes=[pltpu.VMEM((2, rows, CH), BF16)],
        compiler_params=params(24),
        cost_estimate=cost(2 * 1811939328, 12 << 20),
        name="weight_terms",
    )(core, g, x9, sums)


def join_kernel(keep_ref, got_ref, out_ref):
    for k in range(16):
        rows = slice(k * MAIN, (k + 1) * MAIN)
        out_ref[k, 0:MAIN, :] = (keep_ref[rows, :].astype(F32) + got_ref[rows, :].astype(F32)).astype(BF16)
    rows = slice(16 * MAIN, 16 * MAIN + EXTRA)
    ones, sums = unpack(keep_ref[rows, :].astype(F32), 14)
    more_ones, more_sums = unpack(got_ref[rows, :].astype(F32), 14)
    extra = pack(ones + more_ones, sums + more_sums)
    for k in range(16):
        out_ref[k, MAIN : MAIN + EXTRA, :] = extra


def join(keep, got):
    return pl.pallas_call(
        join_kernel,
        out_shape=shape((16, MAIN + EXTRA, CH), BF16),
        in_specs=[VM, VM],
        out_specs=VM,
        compiler_params=params(),
        cost_estimate=cost(1 << 20, 3 << 20),
        name="join",
    )(keep, got)


def middle_kernel(parts_ref, out_ref):
    extra = None
    for k in range(16):
        ones, sums = unpack(parts_ref[k, MAIN : MAIN + EXTRA, :].astype(F32), 14)
        extra = (ones, sums) if extra is None else (extra[0] + ones, extra[1] + sums)
    for z in range(8):
        if z < 7:
            total = None
            for k in range(16):
                term = parts_ref[k, 32 * z : 32 * (z + 1), :].astype(F32)
                total = term if total is None else total + term
            ones = extra[0][2 * z : 2 * z + 2]
        else:
            total, ones = jnp.zeros((32, CH), F32), jnp.zeros((2, CH), F32)
        out_ref[z, 0:32, :] = total.astype(BF16)
        out_ref[z, 32:48, :] = pack(ones, extra[1])


def middle(parts):
    return pl.pallas_call(
        middle_kernel,
        out_shape=shape((8, 48, CH), BF16),
        in_specs=[VM],
        out_specs=VM,
        compiler_params=params(),
        cost_estimate=cost(1 << 20, 2 << 20),
        name="middle",
    )(parts)


def column(row):
    return jnp.transpose(jnp.broadcast_to(row, (CH, CH)))


def combine_kernel(block_ref, parts_ref, norm_ref, gain_ref, out_ref, tot_ref, gg_ref, sg_ref, coef_ref):
    main, sums, ones = None, None, None
    for z in range(8):
        term = parts_ref[z, 0:32, :].astype(F32)
        term_ones, term_sums = unpack(parts_ref[z, 32:48, :].astype(F32), 2)
        main = term if main is None else main + term
        ones = term_ones if ones is None else ones + term_ones
        sums = term_sums if sums is None else sums + term_sums
    inverse, count = norm_ref[1:2], norm_ref[2:3]
    scale = lax.rsqrt(count)
    tot_ref[...] = jnp.concatenate((sums, jnp.zeros((6, CH), F32)), axis=0)
    sg_ref[...] = sums[0:1] * scale
    gg_ref[...] = sums[1:2] * scale
    coef_ref[0] = column(gain_ref[...] * inverse * scale)
    coef_ref[1] = column(sums[0:1] / count)
    coef_ref[2] = column(sums[1:2] / count)
    mine = pl.ds(pl.multiple_of(block_ref[0] * 8, 8), 8)
    factor, first, second = coef_ref[0, mine, :], coef_ref[1, mine, :], coef_ref[2, mine, :]
    values = []
    for i in range(2):
        base, cross = main[16 * i : 16 * i + 8], main[16 * i + 8 : 16 * i + 16]
        values.append(factor * (base - first * ones[i : i + 1] - second * cross))
    out_ref[...] = jnp.concatenate(values, axis=0).astype(BF16)


def combine(block, parts, norm, gain):
    return pl.pallas_call(
        combine_kernel,
        out_shape=(shape((16, CH), BF16), shape((8, CH), F32), shape((1, CH), F32), shape((1, CH), F32)),
        in_specs=[SM] + [VM] * 3,
        out_specs=(VM,) * 4,
        scratch_shapes=[pltpu.VMEM((3, CH, CH), F32)],
        compiler_params=params(),
        cost_estimate=cost(1 << 20, 1 << 20),
        name="combine",
    )(block, parts, norm, gain)


def grad_kernel(
    sends_ref, tot_ref, norm_ref, gain_ref, conv_ref, ga_ref, mask_ref, out_ref, low_ref, high_ref, *, faces
):
    mean, inverse, count = norm_ref[0:1], norm_ref[1:2], norm_ref[2:3]
    factor = gain_ref[...] * inverse
    for s in range(SLOTS):
        normed = (conv_ref[s] - mean) * inverse
        inner = ga_ref[s] - (tot_ref[0:1] + normed * tot_ref[1:2]) / count
        out_ref[s] = (factor * inner * mask_ref[s].astype(F32)).astype(BF16)
    pick_x(sends_ref, out_ref, low_ref, high_ref, faces)


def grad(sends_x, totals, norm, gain, conv_out, ga, mask, faces):
    return pl.pallas_call(
        functools.partial(grad_kernel, faces=faces),
        out_shape=(shape((SLOTS, VOX, CH), BF16),) + x_shapes(faces),
        in_specs=[SM] + [VM] * 6,
        out_specs=(VM,) * 3,
        compiler_params=params(),
        cost_estimate=cost(4 << 20, 4 << 20),
        name="grad_conv",
    )(sends_x, totals, norm, gain, conv_out, ga, mask)


def finish_kernel(core_ref, mine_ref, other_ref, out_ref):
    for half in (0, 1):
        here = core_ref[0] == half
        for z in range(7):
            pairs = []
            for k in range(16):
                rows = slice(16 * z, 16 * (z + 1))
                pairs.append(jnp.where(here, mine_ref[k, rows, :], other_ref[k, rows, :]).astype(F32))
            for i in range(2):
                tap = 13 * half + 2 * z + i
                if half == 1 and tap == 13:
                    continue
                rows = jnp.concatenate([pair[8 * i : 8 * i + 8] for pair in pairs], axis=0)
                out_ref[tap] = jnp.transpose(rows)


def finish(core, mine, other):
    return pl.pallas_call(
        finish_kernel,
        out_shape=shape((27, CH, CH), F32),
        in_specs=[SM, VM, VM],
        out_specs=VM,
        compiler_params=params(),
        cost_estimate=cost(1 << 20, 3 << 20),
        name="finish",
    )(core, mine, other)


def spread(value, axes):
    size = axis_size(axes)
    return lax.all_to_all(jnp.broadcast_to(value[None], (size,) + value.shape), axes, 0, 0)


def all_sum_parts(value):
    return spread(jnp.sum(spread(value, ("z", "c")), axis=0), CROSS)


def swap(value):
    return lax.ppermute(value, "c", [(0, 1), (1, 0)])


def halo(own, low, high, sends_y, faces):
    xl, xu = neighbours(low, high, ("xh", "y"))
    low, high = pick_y(sends_y, own, xl, xu, faces)
    yl, yu = neighbours(low, high, ("xl", "z", "c"))
    return own, xl, xu, yl, yu


def shards(
    features,
    occupancy,
    counts,
    kernel_map,
    x_send,
    y_send,
    weight,
    norm_gain,
    norm_shift,
    cotangent,
):
    row_map, sends_x, sends_y = kernel_map[0, 0], x_send[0, 0], y_send[0, 0]
    gain, shift = norm_gain.reshape(1, CH), norm_shift.reshape(1, CH)
    core = lax.axis_index("c").reshape(1)
    block = lax.axis_index(CROSS).reshape(1)
    ahead = weight.reshape(3, 9 * CH, CH)
    turned = jnp.transpose(weight[::-1], (0, 2, 1)).reshape(3, 9 * CH, CH)

    def first(faces):
        own, mask, low, high = prepare(counts, sends_x, features[0, 0], occupancy[0, 0], faces)
        table = halo(own, low, high, sends_y, faces)
        conv_out, x9, stats = conv(row_map, *table, ahead, mask, True, faces)
        return conv_out, x9, mask, all_sum_parts(stats)

    def second(conv_out, x9, mask, stats, faces):
        activations, ga, g, sums, norm = act(stats, conv_out, cotangent[0, 0], mask, gain, shift)
        keep, send = wgrad(core, g, x9, sums)
        parts = lax.all_to_all(join(keep, swap(send)), CROSS, 0, 0)
        parts = lax.all_to_all(middle(parts), "z", 0, 0)
        value, totals, gain_grad, shift_grad = combine(block, parts, norm, gain)
        grads, low, high = grad(sends_x, totals, norm, gain, conv_out, ga, mask, faces)
        mine = spread(value, ("z",)).reshape(8 * 16, CH)[: 7 * 16]
        mine = spread(mine, CROSS)
        weight_grad = finish(core, mine, swap(mine))
        table = halo(grads, low, high, sends_y, faces)
        features_grad = conv(row_map, *table, turned, mask, False, faces)
        return activations, features_grad, weight_grad, gain_grad, shift_grad

    state = first(True)
    misfits = jnp.sum(state[3][:, 3, 0])
    activations, features_grad, weight_grad, gain_grad, shift_grad = lax.cond(
        misfits > 0,
        lambda *_: second(*first(False), False),
        lambda *given: second(*given, True),
        *state,
    )
    return (
        activations[None, None],
        features_grad[None, None],
        weight_grad,
        gain_grad.reshape(CH),
        shift_grad.reshape(CH),
    )


def solution(mesh):
    fine = jax.sharding.Mesh(mesh.devices.reshape(2, 4, 2, 8, 2), ("xh", "y", "xl", "z", "c"))
    gx, gy = ("xh", "y"), ("xl", "z", "c")
    tiles = P(gx, gy, None, None, None)
    lists = P(gx, gy, None, None)
    return jax.shard_map(
        shards,
        mesh=fine,
        in_specs=(tiles, lists, P(gx, gy), lists, lists, lists, P(), P(), P(), tiles),
        out_specs=(tiles, tiles, P(), P(), P()),
        check_vma=False,
    )
```

time: 209 us -> 167 us (0.80)
  the two profiles are of different devices: /device:TPU:121 before, /device:TPU:26 now
where the time goes in v2:
time: 167 us; the launch traced here: 166 us
  blocking collectives  70.1 us (42%)
  starting transfers between devices  34.9 us (21%)
  Pallas kernels  29 us (17%)
  waiting for transfers between devices  23.1 us (14%)
  local copies, waits for them, and re-layouts  4.84 us (3%)
  between operations  2.22 us (1%)
    all_to_all x3, blocking collectives, spread(): lax.all_to_all(jnp.broadcast_to(value[None], (size,) + value.shape), axes...  37.6 us
    ppermute x8, starting transfers between devices, neighbours(): return (lax.ppermute(high, axis, up), lax.ppermute(low, axis, down))  29.3 us
    all_to_all x1, blocking collectives, second(): parts = lax.all_to_all(join(keep, swap(send)), CROSS, 0, 0)  21.3 us
    ppermute x8, waiting for transfers between devices, neighbours(): return (lax.ppermute(high, axis, up), lax.ppermute(low, axis, down))  18.6 us
    pallas_call x2, Pallas kernels, conv(): pl.pallas_call(functools.partial(conv_kernel, forward=forward, faces=face...  12.5 us
    all_to_all x1, blocking collectives, second(): parts = lax.all_to_all(middle(parts), 'z', 0, 0)  11.1 us
    pallas_call x1, Pallas kernels, wgrad(): pl.pallas_call(wgrad_kernel, out_shape=(shape((rows, CH), BF16), shape((r...  8.24 us
    all_to_all x1, starting transfers between devices, spread(): lax.all_to_all(jnp.broadcast_to(value[None], (size,) + value.shape), axes...  5.43 us
  transfers between devices with their start and end apart: 11, of which 6 were waited for; matrix products, arithmetic and copies ran while one was open for 2% of the time, Pallas kernels for 5%

profile of v2, /device:TPU:26, one launch (start us, length us, event | category | flops | bytes accessed | tf_op | source)
XLA Modules:
  0.0 165.9 jit_solution(14435745711306707968)
XLA Ops:
  0.6 0.0 copy-start.5
  1.4 1.4 prepare.3
  2.8 3.7 %collective-permute-start.16 = (bf16[2,64,128]{2,1,0:T(8,128)(2,1)S(1)}, bf16[2,64,128]{2,1,0:T(8,128)(2,1)S(1)}, u32[]{:S(2)}, u32[]{:S(2)}) collective-permute-start(bf16[2,64,128]{2,1,0:T(8,128)(2,1)S(1)} %get-tuple-element.140), channel_id=1, source_target_pairs={{0,32},{32,64},{64,96},{96,128},{128,160},{160,192},{192,224},{1,3... | collective-permute-start | bytes 98312 | tf_op jit(solution)/shard_map/ppermute | solution.py:174
  6.5 2.2 %collective-permute-start.17 = (bf16[2,64,128]{2,1,0:T(8,128)(2,1)S(1)}, bf16[2,64,128]{2,1,0:T(8,128)(2,1)S(1)}, u32[]{:S(2)}, u32[]{:S(2)}) collective-permute-start(bf16[2,64,128]{2,1,0:T(8,128)(2,1)S(1)} %get-tuple-element.141), channel_id=1, source_target_pairs={{32,0},{64,32},{96,64},{128,96},{160,128},{192,160},{224,192},{33,... | collective-permute-start | bytes 98312 | tf_op jit(solution)/shard_map/ppermute | solution.py:174
  8.7 7.3 %collective-permute-done.17.xu_ref = bf16[2,64,128]{2,1,0:T(8,128)(2,1)S(1)} collective-permute-done((bf16[2,64,128]{2,1,0:T(8,128)(2,1)S(1)}, bf16[2,64,128]{2,1,0:T(8,128)(2,1)S(1)}, u32[]{:S(2)}, u32[]{:S(2)}) %collective-permute-start.17) | collective-permute-done | bytes 32800 | tf_op jit(solution)/shard_map/ppermute | solution.py:174
  15.9 0.9 pick_y.7
  16.8 1.9 %collective-permute-start.18 = (bf16[272,128]{1,0:T(8,128)(2,1)S(1)}, bf16[272,128]{1,0:T(8,128)(2,1)S(1)}, u32[]{:S(2)}, u32[]{:S(2)}) collective-permute-start(bf16[272,128]{1,0:T(8,128)(2,1)S(1)} %get-tuple-element.142), channel_id=1, source_target_pairs={{0,1},{1,2},{2,3},{3,4},{4,5},{5,6},{6,7},{7,8},{8,9},{9,10},{10,1... | collective-permute-start | bytes 208904 | tf_op jit(solution)/shard_map/ppermute | solution.py:174
  18.7 6.7 %collective-permute-start.19 = (bf16[272,128]{1,0:T(8,128)(2,1)S(1)}, bf16[272,128]{1,0:T(8,128)(2,1)S(1)}, u32[]{:S(2)}, u32[]{:S(2)}) collective-permute-start(bf16[272,128]{1,0:T(8,128)(2,1)S(1)} %get-tuple-element.143), channel_id=1, source_target_pairs={{1,0},{2,1},{3,2},{4,3},{5,4},{6,5},{7,6},{8,7},{9,8},{10,9},{11,1... | collective-permute-start | bytes 208904 | tf_op jit(solution)/shard_map/ppermute | solution.py:174
  25.4 0.1 collective-permute-done.18.yl_ref
  25.4 1.9 %collective-permute-done.19.yu_ref = bf16[272,128]{1,0:T(8,128)(2,1)S(1)} collective-permute-done((bf16[272,128]{1,0:T(8,128)(2,1)S(1)}, bf16[272,128]{1,0:T(8,128)(2,1)S(1)}, u32[]{:S(2)}, u32[]{:S(2)}) %collective-permute-start.19) | collective-permute-done | bytes 69664 | tf_op jit(solution)/shard_map/ppermute | solution.py:174
  27.3 6.5 %forward_conv.3 = (f32[4,512,128]{2,1,0:T(8,128)S(1)}, bf16[4,640,1152]{2,1,0:T(8,128)(2,1)}, f32[8,128]{1,0:T(8,128)S(1)}) custom-call(s32[4,27]{1,0:T(4,128)S(1)} %bitcast.46, s32[4,27]{1,0:T(4,128)S(1)} %bitcast.47, bf16[4,512,128]{2,1,0:T(8,128)(2,1)S(1)} %get-tuple-element.139.own_ref, bf16[2,64,128]{2,1,0:T(8,128)(2,1)S(1)} %collective-permute-done.16.xl_ref, ...), custom_call_target="tpu_custom_call" | custom-call | flops 1811939328 | bytes 12582912 | tf_op jit(solution)/shard_map/forward_conv/pallas_call | solution.py:304
  33.8 14.8 %all_to_all.59 = f32[16,8,128]{2,1,0:T(8,128)S(1)} all-to-all(f32[16,8,128]{2,1,0:T(8,128)S(1)} %broadcast_in_dim.36), channel_id=1, replica_groups=mesh['xh'=2,'y'=4,'xl'=2,'z'=8,'c'=2] {'z','c'}, dimensions={0} | all-to-all | bytes 131072 | tf_op jit(solution)/shard_map/all_to_all | solution.py:610
  48.6 0.6 broadcast_in_dim.37
  49.2 5.4 %all-to-all-start.11 = ((f32[16,8,128]{2,1,0:T(8,128)}), f32[16,8,128]{2,1,0:T(8,128)}, u32[]{:S(2)}, u32[]{:S(2)}) async-start(f32[16,8,128]{2,1,0:T(8,128)} %broadcast_in_dim.37), calls=%async_computation.11 | async-start | bytes 131072 | tf_op jit(solution)/shard_map/all_to_all | solution.py:610
  54.6 1.2 reverse_bitcast_fusion
  55.8 0.0 copy-start.2
  55.9 0.0 copy-start.3
  55.9 0.0 copy-start.8
  55.9 0.0 copy-start.10
  55.9 0.0 copy-start.11
  55.9 1.6 copy.16
  57.6 2.0 %all-to-all-done.11 = f32[16,8,128]{2,1,0:T(8,128)} async-done(((f32[16,8,128]{2,1,0:T(8,128)}), f32[16,8,128]{2,1,0:T(8,128)}, u32[]{:S(2)}, u32[]{:S(2)}) %all-to-all-start.11) | async-done | bytes 65568 | tf_op jit(solution)/shard_map/all_to_all | solution.py:610
  59.6 1.5 slice_reduce_fusion
  61.8 102.9 %conditional.1 = (bf16[4,512,128]{2,1,0:T(8,128)(2,1)}, f32[27,128,128]{2,1,0:T(8,128)S(1)}, f32[1,128]{1,0:T(1,128)}, f32[1,128]{1,0:T(1,128)}, bf16[1,1,4,512,128]{4,3,2,1,0:T(8,128)(2,1)}) conditional(s32[]{:T(128)} %convert_element_type.3, (bf16[1,1,4,512,128]{4,3,2,1,0:T(8,128)(2,1)S(1)}, f32[16,8,128]{2,1,0:T(8,128)}, ...), branch_computations={%region_2.0_spmd, %region_3.0_spmd} | conditional | flops 7267695616 | bytes 136696352 | solution.py:669
  61.8 3.0 %activation.2 = (bf16[4,512,128]{2,1,0:T(8,128)(2,1)}, f32[4,512,128]{2,1,0:T(8,128)S(1)}, bf16[4,272,512]{2,1,0:T(8,128)(2,1)S(1)}, f32[8,128]{1,0:T(8,128)S(1)}, f32[8,128]{1,0:T(8,128)S(1)}) custom-call(f32[16,8,128]{2,1,0:T(8,128)} %get-tuple-element.53.stat_ref, f32[4,512,128]{2,1,0:T(8,128)S(1)} %get-tuple-element.54.conv_ref, ...), custom_call_target="tpu_custom_call" | custom-call | flops 8388608 | bytes 5242880 | tf_op jit(solution)/shard_map/cond/branch_0_fun/activation/pallas_call | solution.py:362
  64.8 8.2 %weight_terms.2 = (bf16[3632,128]{1,0:T(8,128)(2,1)S(1)}, bf16[3632,128]{1,0:T(8,128)(2,1)S(1)}) custom-call(s32[1]{0:T(128)} %get-tuple-element.60.core_ref, bf16[4,272,512]{2,1,0:T(8,128)(2,1)S(1)} %get-tuple-element.62.g_ref, bf16[4,640,1152]{2,1,0:T(8,128)(2,1)} %get-tuple-element.63.x9_ref, f32[8,128]{1,0:T(8,128)S(1)} %get-tuple-element.64.sum_ref), custom_call_target="tpu_custom_call" | custom-call | flops 3623878656 | bytes 12582912 | tf_op jit(solution)/shard_map/cond/branch_0_fun/weight_terms/pallas_call | solution.py:448
  73.0 0.1 collective-permute-start
  73.1 2.5 %collective-permute-done.got_ref = bf16[3632,128]{1,0:T(8,128)(2,1)S(1)} collective-permute-done((bf16[3632,128]{1,0:T(8,128)(2,1)S(1)}, bf16[3632,128]{1,0:T(8,128)(2,1)S(1)}, u32[]{:S(2)}, u32[]{:S(2)}) %collective-permute-start) | collective-permute-done | bytes 929824 | tf_op jit(solution)/shard_map/cond/branch_0_fun/ppermute | solution.py:618
  75.6 0.2 join.2
  75.8 21.3 %all_to_all.50.parts_ref = bf16[16,272,128]{2,1,0:T(8,128)(2,1)S(1)} all-to-all(bf16[16,272,128]{2,1,0:T(8,128)(2,1)S(1)} %join.2), channel_id=1, replica_groups=mesh['xh'=2,'y'=4,'xl'=2,'z'=8,'c'=2] {'xh','y','xl'}, dimensions={0} | all-to-all | bytes 2228224 | tf_op jit(solution)/shard_map/cond/branch_0_fun/all_to_all | solution.py:656
  97.2 0.2 middle.2
  97.4 11.1 %all_to_all.51.parts_ref = bf16[8,48,128]{2,1,0:T(8,128)(2,1)S(1)} all-to-all(bf16[8,48,128]{2,1,0:T(8,128)(2,1)S(1)} %middle.2), channel_id=1, replica_groups=mesh['xh'=2,'y'=4,'xl'=2,'z'=8,'c'=2] {'z'}, dimensions={0} | all-to-all | bytes 196608 | tf_op jit(solution)/shard_map/cond/branch_0_fun/all_to_all | solution.py:657
  108.5 0.5 combine.2
  109.0 10.4 %all_to_all.52 = bf16[8,16,128]{2,1,0:T(8,128)(2,1)S(1)} all-to-all(bf16[8,16,128]{2,1,0:T(8,128)(2,1)S(1)} %broadcast_in_dim.13), channel_id=1, replica_groups=mesh['xh'=2,'y'=4,'xl'=2,'z'=8,'c'=2] {'z'}, dimensions={0} | all-to-all | bytes 65536 | tf_op jit(solution)/shard_map/cond/branch_0_fun/all_to_all | solution.py:610
  119.4 0.1 broadcast_in_dim.15
  119.4 12.5 %all_to_all.53.mine_ref = bf16[16,112,128]{2,1,0:T(8,128)(2,1)S(1)} all-to-all(bf16[16,112,128]{2,1,0:T(8,128)(2,1)S(1)} %broadcast_in_dim.15), channel_id=1, replica_groups=mesh['xh'=2,'y'=4,'xl'=2,'z'=8,'c'=2] {'xh','y','xl'}, dimensions={0} | all-to-all | bytes 917504 | tf_op jit(solution)/shard_map/cond/branch_0_fun/all_to_all | solution.py:610
  131.9 1.1 grad_conv.2
  133.0 5.3 %collective-permute-start.2 = (bf16[2,64,128]{2,1,0:T(8,128)(2,1)S(1)}, bf16[2,64,128]{2,1,0:T(8,128)(2,1)S(1)}, u32[]{:S(2)}, u32[]{:S(2)}) collective-permute-start(bf16[2,64,128]{2,1,0:T(8,128)(2,1)S(1)} %get-tuple-element.76), channel_id=1, source_target_pairs={{0,32},{32,64},{64,96},{96,128},{128,160},{160,192},{192,224},{1,3... | collective-permute-start | bytes 98312 | tf_op jit(solution)/shard_map/cond/branch_0_fun/ppermute | solution.py:174
  138.4 1.9 %collective-permute-start.3 = (bf16[2,64,128]{2,1,0:T(8,128)(2,1)S(1)}, bf16[2,64,128]{2,1,0:T(8,128)(2,1)S(1)}, u32[]{:S(2)}, u32[]{:S(2)}) collective-permute-start(bf16[2,64,128]{2,1,0:T(8,128)(2,1)S(1)} %get-tuple-element.77), channel_id=1, source_target_pairs={{32,0},{64,32},{96,64},{128,96},{160,128},{192,160},{224,192},{33,... | collective-permute-start | bytes 98312 | tf_op jit(solution)/shard_map/cond/branch_0_fun/ppermute | solution.py:174
  140.3 7.5 %collective-permute-done.3.xu_ref = bf16[2,64,128]{2,1,0:T(8,128)(2,1)S(1)} collective-permute-done((bf16[2,64,128]{2,1,0:T(8,128)(2,1)S(1)}, bf16[2,64,128]{2,1,0:T(8,128)(2,1)S(1)}, u32[]{:S(2)}, u32[]{:S(2)}) %collective-permute-start.3) | collective-permute-done | bytes 32800 | tf_op jit(solution)/shard_map/cond/branch_0_fun/ppermute | solution.py:174
  147.8 0.7 pick_y.4
  148.5 1.9 %collective-permute-start.4 = (bf16[272,128]{1,0:T(8,128)(2,1)S(1)}, bf16[272,128]{1,0:T(8,128)(2,1)S(1)}, u32[]{:S(2)}, u32[]{:S(2)}) collective-permute-start(bf16[272,128]{1,0:T(8,128)(2,1)S(1)} %get-tuple-element.79), channel_id=1, source_target_pairs={{0,1},{1,2},{2,3},{3,4},{4,5},{5,6},{6,7},{7,8},{8,9},{9,10},{10,1... | collective-permute-start | bytes 208904 | tf_op jit(solution)/shard_map/cond/branch_0_fun/ppermute | solution.py:174
  150.4 5.8 %collective-permute-start.5 = (bf16[272,128]{1,0:T(8,128)(2,1)S(1)}, bf16[272,128]{1,0:T(8,128)(2,1)S(1)}, u32[]{:S(2)}, u32[]{:S(2)}) collective-permute-start(bf16[272,128]{1,0:T(8,128)(2,1)S(1)} %get-tuple-element.80), channel_id=1, source_target_pairs={{1,0},{2,1},{3,2},{4,3},{5,4},{6,5},{7,6},{8,7},{9,8},{10,9},{11,1... | collective-permute-start | bytes 208904 | tf_op jit(solution)/shard_map/cond/branch_0_fun/ppermute | solution.py:174
  156.2 0.1 collective-permute-done.4.yl_ref
  156.2 1.9 %collective-permute-done.5.yu_ref = bf16[272,128]{1,0:T(8,128)(2,1)S(1)} collective-permute-done((bf16[272,128]{1,0:T(8,128)(2,1)S(1)}, bf16[272,128]{1,0:T(8,128)(2,1)S(1)}, u32[]{:S(2)}, u32[]{:S(2)}) %collective-permute-start.5) | collective-permute-done | bytes 69664 | tf_op jit(solution)/shard_map/cond/branch_0_fun/ppermute | solution.py:174
  158.1 6.0 %transposed_conv.2 = bf16[4,512,128]{2,1,0:T(8,128)(2,1)} custom-call(s32[4,27]{1,0:T(4,128)S(1)} %get-tuple-element.71.map_ref.rows_ref, s32[4,27]{1,0:T(4,128)S(1)} %get-tuple-element.71.map_ref.rows_ref, bf16[4,512,128]{2,1,0:T(8,128)(2,1)S(1)} %get-tuple-element.75.own_ref, bf16[2,64,128]{2,1,0:T(8,128)(2,1)S(1)} %collective-permute-done.2.xl_ref, ...), custom_call_target="tpu_custom_call" | custom-call | flops 1811939328 | bytes 12582912 | tf_op jit(solution)/shard_map/cond/branch_0_fun/transposed_conv/pallas_call | solution.py:304
  164.1 0.4 finish.2
  164.7 1.2 copy-done.4
  (23 shorter events, 0.1 us)
Async XLA Ops:
  0.6 26.7 %copy-start.5 = (bf16[27,128,128]{2,1,0:T(8,128)(2,1)S(1)}, bf16[27,128,128]{2,1,0:T(8,128)(2,1)}, u32[]{:S(2)}) copy-start(bf16[27,128,128]{2,1,0:T(8,128)(2,1)} %param.18) | copy-start | bytes 2654212
  0.6 26.7 %copy-start.13 = (s32[1,1,4,27]{3,2,1,0:T(4,128)S(1)}, s32[1,1,4,27]{3,2,1,0:T(4,128)}, u32[]{:S(2)}) copy-start(s32[1,1,4,27]{3,2,1,0:T(4,128)} %param.15) | copy-start | bytes 1300
  2.8 5.9 %collective-permute-start.16 = (bf16[2,64,128]{2,1,0:T(8,128)(2,1)S(1)}, bf16[2,64,128]{2,1,0:T(8,128)(2,1)S(1)}, u32[]{:S(2)}, u32[]{:S(2)}) collective-permute-start(bf16[2,64,128]{2,1,0:T(8,128)(2,1)S(1)} %get-tuple-element.140), channel_id=1, source_target_pairs={{0,32},{32,64},{64,96},{96,128},{128,160},{160,192},{192,224},{1,3... | collective-permute-start | bytes 98312 | tf_op jit(solution)/shard_map/ppermute | solution.py:174
  6.5 9.4 %collective-permute-start.17 = (bf16[2,64,128]{2,1,0:T(8,128)(2,1)S(1)}, bf16[2,64,128]{2,1,0:T(8,128)(2,1)S(1)}, u32[]{:S(2)}, u32[]{:S(2)}) collective-permute-start(bf16[2,64,128]{2,1,0:T(8,128)(2,1)S(1)} %get-tuple-element.141), channel_id=1, source_target_pairs={{32,0},{64,32},{96,64},{128,96},{160,128},{192,160},{224,192},{33,... | collective-permute-start | bytes 98312 | tf_op jit(solution)/shard_map/ppermute | solution.py:174
  16.8 8.6 %collective-permute-start.18 = (bf16[272,128]{1,0:T(8,128)(2,1)S(1)}, bf16[272,128]{1,0:T(8,128)(2,1)S(1)}, u32[]{:S(2)}, u32[]{:S(2)}) collective-permute-start(bf16[272,128]{1,0:T(8,128)(2,1)S(1)} %get-tuple-element.142), channel_id=1, source_target_pairs={{0,1},{1,2},{2,3},{3,4},{4,5},{5,6},{6,7},{7,8},{8,9},{9,10},{10,1... | collective-permute-start | bytes 208904 | tf_op jit(solution)/shard_map/ppermute | solution.py:174
  18.7 8.6 %collective-permute-start.19 = (bf16[272,128]{1,0:T(8,128)(2,1)S(1)}, bf16[272,128]{1,0:T(8,128)(2,1)S(1)}, u32[]{:S(2)}, u32[]{:S(2)}) collective-permute-start(bf16[272,128]{1,0:T(8,128)(2,1)S(1)} %get-tuple-element.143), channel_id=1, source_target_pairs={{1,0},{2,1},{3,2},{4,3},{5,4},{6,5},{7,6},{8,7},{9,8},{10,9},{11,1... | collective-permute-start | bytes 208904 | tf_op jit(solution)/shard_map/ppermute | solution.py:174
  49.2 10.4 %all-to-all-start.11 = ((f32[16,8,128]{2,1,0:T(8,128)}), f32[16,8,128]{2,1,0:T(8,128)}, u32[]{:S(2)}, u32[]{:S(2)}) async-start(f32[16,8,128]{2,1,0:T(8,128)} %broadcast_in_dim.37), calls=%async_computation.11 | async-start | bytes 131072 | tf_op jit(solution)/shard_map/all_to_all | solution.py:610
  55.8 5.9 %copy-start.2 = (bf16[1,1,4,512,128]{4,3,2,1,0:T(8,128)(2,1)S(1)}, bf16[1,1,4,512,128]{4,3,2,1,0:T(8,128)(2,1)}, u32[]{:S(2)}) copy-start(bf16[1,1,4,512,128]{4,3,2,1,0:T(8,128)(2,1)} %param.12) | copy-start | bytes 1572868
  55.9 5.9 %copy-start.3 = (bf16[1,1,4,512,128]{4,3,2,1,0:T(8,128)(2,1)S(1)}, bf16[1,1,4,512,128]{4,3,2,1,0:T(8,128)(2,1)}, u32[]{:S(2)}) copy-start(bf16[1,1,4,512,128]{4,3,2,1,0:T(8,128)(2,1)} %param.21) | copy-start | bytes 1572868
  55.9 5.9 %copy-start.8 = (s32[1,1,4,512]{3,2,1,0:T(4,128)S(1)}, s32[1,1,4,512]{3,2,1,0:T(4,128)}, u32[]{:S(2)}) copy-start(s32[1,1,4,512]{3,2,1,0:T(4,128)} %param.13) | copy-start | bytes 24580
  55.9 5.9 %copy-start.9 = (f32[128]{0:T(128)S(1)}, f32[128]{0:T(128)}, u32[]{:S(2)}) copy-start(f32[128]{0:T(128)} %param.19) | copy-start | bytes 1540
  55.9 5.9 %copy-start.10 = (s32[1,1,2,2]{3,2,1,0:T(2,128)S(1)}, s32[1,1,2,2]{3,2,1,0:T(2,128)}, u32[]{:S(2)}) copy-start(s32[1,1,2,2]{3,2,1,0:T(2,128)} %param.16) | copy-start | bytes 52
  55.9 5.9 %copy-start.11 = (s32[1,1,2,4]{3,2,1,0:T(2,128)S(1)}, s32[1,1,2,4]{3,2,1,0:T(2,128)}, u32[]{:S(2)}) copy-start(s32[1,1,2,4]{3,2,1,0:T(2,128)} %param.17) | copy-start | bytes 100
  55.9 5.9 %copy-start.12 = (f32[128]{0:T(128)S(1)}, f32[128]{0:T(128)}, u32[]{:S(2)}) copy-start(f32[128]{0:T(128)} %param.20) | copy-start | bytes 1540
  73.0 2.6 %collective-permute-start = (bf16[3632,128]{1,0:T(8,128)(2,1)S(1)}, bf16[3632,128]{1,0:T(8,128)(2,1)S(1)}, u32[]{:S(2)}, u32[]{:S(2)}) collective-permute-start(bf16[3632,128]{1,0:T(8,128)(2,1)S(1)} %get-tuple-element.66), channel_id=1, source_target_pairs={{0,1},{1,0},{2,3},{3,2},{4,5},{5,4},{6,7},{7,6},{8,9},{9,8},{10,11... | collective-permute-start | bytes 2789384 | tf_op jit(solution)/shard_map/cond/branch_0_fun/ppermute | solution.py:618
  131.9 32.2 %collective-permute-start.1 = (bf16[16,112,128]{2,1,0:T(8,128)(2,1)S(1)}, bf16[16,112,128]{2,1,0:T(8,128)(2,1)S(1)}, u32[]{:S(2)}, u32[]{:S(2)}) collective-permute-start(bf16[16,112,128]{2,1,0:T(8,128)(2,1)S(1)} %all_to_all.53.mine_ref), channel_id=1, source_target_pairs={{0,1},{1,0},{2,3},{3,2},{4,5},{5,4},{6,7},{7,6},{8,9},{9,8},{10,11... | collective-permute-start | bytes 1376264 | tf_op jit(solution)/shard_map/cond/branch_0_fun/ppermute | solution.py:618
  131.9 26.2 %copy-start.7 = (bf16[3,1152,128]{2,1,0:T(8,128)(2,1)S(1)}, bf16[3,1152,128]{2,1,0:T(8,128)(2,1)}, u32[]{:S(2)}) copy-start(bf16[3,1152,128]{2,1,0:T(8,128)(2,1)} %get-tuple-element.81.w_ref) | copy-start | bytes 2654212 | tf_op jit(solution)/shard_map/cond
  133.0 7.3 %collective-permute-start.2 = (bf16[2,64,128]{2,1,0:T(8,128)(2,1)S(1)}, bf16[2,64,128]{2,1,0:T(8,128)(2,1)S(1)}, u32[]{:S(2)}, u32[]{:S(2)}) collective-permute-start(bf16[2,64,128]{2,1,0:T(8,128)(2,1)S(1)} %get-tuple-element.76), channel_id=1, source_target_pairs={{0,32},{32,64},{64,96},{96,128},{128,160},{160,192},{192,224},{1,3... | collective-permute-start | bytes 98312 | tf_op jit(solution)/shard_map/cond/branch_0_fun/ppermute | solution.py:174
  138.4 9.4 %collective-permute-start.3 = (bf16[2,64,128]{2,1,0:T(8,128)(2,1)S(1)}, bf16[2,64,128]{2,1,0:T(8,128)(2,1)S(1)}, u32[]{:S(2)}, u32[]{:S(2)}) collective-permute-start(bf16[2,64,128]{2,1,0:T(8,128)(2,1)S(1)} %get-tuple-element.77), channel_id=1, source_target_pairs={{32,0},{64,32},{96,64},{128,96},{160,128},{192,160},{224,192},{33,... | collective-permute-start | bytes 98312 | tf_op jit(solution)/shard_map/cond/branch_0_fun/ppermute | solution.py:174
  148.5 7.7 %collective-permute-start.4 = (bf16[272,128]{1,0:T(8,128)(2,1)S(1)}, bf16[272,128]{1,0:T(8,128)(2,1)S(1)}, u32[]{:S(2)}, u32[]{:S(2)}) collective-permute-start(bf16[272,128]{1,0:T(8,128)(2,1)S(1)} %get-tuple-element.79), channel_id=1, source_target_pairs={{0,1},{1,2},{2,3},{3,4},{4,5},{5,6},{6,7},{7,8},{8,9},{9,10},{10,1... | collective-permute-start | bytes 208904 | tf_op jit(solution)/shard_map/cond/branch_0_fun/ppermute | solution.py:174
  150.4 7.7 %collective-permute-start.5 = (bf16[272,128]{1,0:T(8,128)(2,1)S(1)}, bf16[272,128]{1,0:T(8,128)(2,1)S(1)}, u32[]{:S(2)}, u32[]{:S(2)}) collective-permute-start(bf16[272,128]{1,0:T(8,128)(2,1)S(1)} %get-tuple-element.80), channel_id=1, source_target_pairs={{1,0},{2,1},{3,2},{4,3},{5,4},{6,5},{7,6},{8,7},{9,8},{10,9},{11,1... | collective-permute-start | bytes 208904 | tf_op jit(solution)/shard_map/cond/branch_0_fun/ppermute | solution.py:174
  164.7 1.2 copy-start.4

commit v3 on v2

--- a/solution.py
+++ b/solution.py
@@ -319,7 +319,7 @@
         out_specs=out_specs,
         scratch_shapes=scratch,
         compiler_params=params(24),
-        cost_estimate=cost(1811939328, 12 << 20),
+        cost_estimate=cost(6000000000, 12 << 20),
         name="forward_conv" if forward else "transposed_conv",
     )(row_map, row_map, own, xl, xu, yl, yu, weight, mask)
 
@@ -409,7 +409,7 @@
     return ones, jnp.concatenate((first, second), axis=0)
 
 
-def wgrad_kernel(core_ref, g_ref, x9_ref, sum_ref, keep_ref, send_ref, full_ref):
+def wgrad_kernel(core_ref, g_ref, x9_ref, sum_ref, keep_ref, send_ref, hold_ref):
     ones = [None] * 27
     for p in range(3):
         for q in range(3):
@@ -434,23 +434,23 @@
                                 (tap[8 * k : 8 * k + 8], tap[CH + 8 * k : CH + 8 * k + 8]), axis=0
                             )
                             row = k * MAIN + i * 16
-                            full_ref[half, row : row + 16, :] = pair.astype(BF16)
+                            hold_ref[half, row : row + 16, :] = pair
     for half in (0, 1):
         rows = jnp.concatenate(ones[13 * half : 13 * half + 14], axis=0)
-        full_ref[half, 16 * MAIN : 16 * MAIN + EXTRA, :] = pack(rows, sum_ref[0:2])
+        hold_ref[half, 16 * MAIN : 16 * MAIN + EXTRA, :] = pack(rows, sum_ref[0:2]).astype(F32)
     core = core_ref[0]
-    keep_ref[...] = full_ref[core]
-    send_ref[...] = full_ref[1 - core]
+    keep_ref[...] = hold_ref[core]
+    send_ref[...] = hold_ref[1 - core].astype(BF16)
 
 
 def wgrad(core, g, x9, sums):
     rows = 16 * MAIN + EXTRA
     return pl.pallas_call(
         wgrad_kernel,
-        out_shape=(shape((rows, CH), BF16), shape((rows, CH), BF16)),
+        out_shape=(shape((rows, CH), F32), shape((rows, CH), BF16)),
         in_specs=[SM, VM, VM, VM],
         out_specs=(VM, VM),
-        scratch_shapes=[pltpu.VMEM((2, rows, CH), BF16)],
+        scratch_shapes=[pltpu.VMEM((2, rows, CH), F32)],
         compiler_params=params(24),
         cost_estimate=cost(2 * 1811939328, 12 << 20),
         name="weight_terms",
@@ -460,9 +460,9 @@
 def join_kernel(keep_ref, got_ref, out_ref):
     for k in range(16):
         rows = slice(k * MAIN, (k + 1) * MAIN)
-        out_ref[k, 0:MAIN, :] = (keep_ref[rows, :].astype(F32) + got_ref[rows, :].astype(F32)).astype(BF16)
+        out_ref[k, 0:MAIN, :] = (keep_ref[rows, :] + got_ref[rows, :].astype(F32)).astype(BF16)
     rows = slice(16 * MAIN, 16 * MAIN + EXTRA)
-    ones, sums = unpack(keep_ref[rows, :].astype(F32), 14)
+    ones, sums = unpack(keep_ref[rows, :], 14)
     more_ones, more_sums = unpack(got_ref[rows, :].astype(F32), 14)
     extra = pack(ones + more_ones, sums + more_sums)
     for k in range(16):
@@ -495,14 +495,13 @@
             ones = extra[0][2 * z : 2 * z + 2]
         else:
             total, ones = jnp.zeros((32, CH), F32), jnp.zeros((2, CH), F32)
-        out_ref[z, 0:32, :] = total.astype(BF16)
-        out_ref[z, 32:48, :] = pack(ones, extra[1])
+        out_ref[z] = jnp.concatenate((total, ones, extra[1], jnp.zeros((4, CH), F32)), axis=0)
 
 
 def middle(parts):
     return pl.pallas_call(
         middle_kernel,
-        out_shape=shape((8, 48, CH), BF16),
+        out_shape=shape((8, 40, CH), F32),
         in_specs=[VM],
         out_specs=VM,
         compiler_params=params(),
@@ -516,13 +515,8 @@
 
 
 def combine_kernel(block_ref, parts_ref, norm_ref, gain_ref, out_ref, tot_ref, gg_ref, sg_ref, coef_ref):
-    main, sums, ones = None, None, None
-    for z in range(8):
-        term = parts_ref[z, 0:32, :].astype(F32)
-        term_ones, term_sums = unpack(parts_ref[z, 32:48, :].astype(F32), 2)
-        main = term if main is None else main + term
-        ones = term_ones if ones is None else ones + term_ones
-        sums = term_sums if sums is None else sums + term_sums
+    total = jnp.sum(parts_ref[...], axis=0)
+    main, ones, sums = total[0:32], total[32:34], total[34:36]
     inverse, count = norm_ref[1:2], norm_ref[2:3]
     scale = lax.rsqrt(count)
     tot_ref[...] = jnp.concatenate((sums, jnp.zeros((6, CH), F32)), axis=0)
@@ -657,11 +651,16 @@
         parts = lax.all_to_all(middle(parts), "z", 0, 0)
         value, totals, gain_grad, shift_grad = combine(block, parts, norm, gain)
         grads, low, high = grad(sends_x, totals, norm, gain, conv_out, ga, mask, faces)
+        value, low, high = lax.optimization_barrier((value, low, high))
+        xl, xu = neighbours(low, high, ("xh", "y"))
         mine = spread(value, ("z",)).reshape(8 * 16, CH)[: 7 * 16]
+        low, high = pick_y(sends_y, grads, xl, xu, faces)
+        mine, low, high = lax.optimization_barrier((mine, low, high))
+        yl, yu = neighbours(low, high, ("xl", "z", "c"))
         mine = spread(mine, CROSS)
+        features_grad = conv(row_map, grads, xl, xu, yl, yu, turned, mask, False, faces)
+        mine, features_grad = lax.optimization_barrier((mine, features_grad))
         weight_grad = finish(core, mine, swap(mine))
-        table = halo(grads, low, high, sends_y, faces)
-        features_grad = conv(row_map, *table, turned, mask, False, faces)
         return activations, features_grad, weight_grad, gain_grad, shift_grad
 
     state = first(True)

time: 167 us -> 159 us (0.952)
  the two profiles are of different devices: /device:TPU:26 before, /device:TPU:1 now
where the time goes in v3:
time: 159 us
  starting transfers between devices  51.4 us (32%)
  blocking collectives  46.9 us (29%)
  Pallas kernels  29.6 us (19%)
  waiting for transfers between devices  20.3 us (13%)
  local copies, waits for them, and re-layouts  6.3 us (4%)
  between operations  2.16 us (1%)
    ppermute x8, starting transfers between devices, neighbours(): return (lax.ppermute(high, axis, up), lax.ppermute(low, axis, down))  25.4 us
    all_to_all x3, starting transfers between devices, spread(): lax.all_to_all(jnp.broadcast_to(value[None], (size,) + value.shape), axes...  20.6 us
    all_to_all x1, blocking collectives, second(): parts = lax.all_to_all(join(keep, swap(send)), CROSS, 0, 0)  20.1 us
    all_to_all x1, blocking collectives, spread(): lax.all_to_all(jnp.broadcast_to(value[None], (size,) + value.shape), axes...  16.1 us
    pallas_call x2, Pallas kernels, conv(): pl.pallas_call(functools.partial(conv_kernel, forward=forward, faces=face...  13.1 us
    all_to_all x1, blocking collectives, second(): parts = lax.all_to_all(middle(parts), 'z', 0, 0)  10.8 us
    ppermute x8, waiting for transfers between devices, neighbours(): return (lax.ppermute(high, axis, up), lax.ppermute(low, axis, down))  10.7 us
    pallas_call x1, Pallas kernels, wgrad(): pl.pallas_call(wgrad_kernel, out_shape=(shape((rows, CH), F32), shape((ro...  8.22 us
  transfers between devices with their start and end apart: 13, of which 7 were waited for; matrix products, arithmetic and copies ran while one was open for 2% of the time, Pallas kernels for 4%

profile of v3, /device:TPU:1, one launch (start us, length us, event | category | flops | bytes accessed | tf_op | source)
XLA Modules:
  0.0 158.5 jit_solution(1231636782918093783)
XLA Ops:
  1.3 1.4 prepare.3
  2.7 4.0 %collective-permute-start.16 = (bf16[2,64,128]{2,1,0:T(8,128)(2,1)S(1)}, bf16[2,64,128]{2,1,0:T(8,128)(2,1)S(1)}, u32[]{:S(2)}, u32[]{:S(2)}) collective-permute-start(bf16[2,64,128]{2,1,0:T(8,128)(2,1)S(1)} %get-tuple-element.155), channel_id=1, source_target_pairs={{0,32},{32,64},{64,96},{96,128},{128,160},{160,192},{192,224},{1,3... | collective-permute-start | bytes 98312 | tf_op jit(solution)/shard_map/ppermute | solution.py:174
  6.7 1.3 collective-permute-start.17
  8.0 3.3 %collective-permute-done.17.xu_ref = bf16[2,64,128]{2,1,0:T(8,128)(2,1)S(1)} collective-permute-done((bf16[2,64,128]{2,1,0:T(8,128)(2,1)S(1)}, bf16[2,64,128]{2,1,0:T(8,128)(2,1)S(1)}, u32[]{:S(2)}, u32[]{:S(2)}) %collective-permute-start.17) | collective-permute-done | bytes 32800 | tf_op jit(solution)/shard_map/ppermute | solution.py:174
  11.4 0.9 pick_y.7
  12.3 5.5 %collective-permute-start.18 = (bf16[272,128]{1,0:T(8,128)(2,1)S(1)}, bf16[272,128]{1,0:T(8,128)(2,1)S(1)}, u32[]{:S(2)}, u32[]{:S(2)}) collective-permute-start(bf16[272,128]{1,0:T(8,128)(2,1)S(1)} %get-tuple-element.157), channel_id=1, source_target_pairs={{0,1},{1,2},{2,3},{3,4},{4,5},{5,6},{6,7},{7,8},{8,9},{9,10},{10,1... | collective-permute-start | bytes 208904 | tf_op jit(solution)/shard_map/ppermute | solution.py:174
  17.8 1.9 %collective-permute-start.19 = (bf16[272,128]{1,0:T(8,128)(2,1)S(1)}, bf16[272,128]{1,0:T(8,128)(2,1)S(1)}, u32[]{:S(2)}, u32[]{:S(2)}) collective-permute-start(bf16[272,128]{1,0:T(8,128)(2,1)S(1)} %get-tuple-element.158), channel_id=1, source_target_pairs={{1,0},{2,1},{3,2},{4,3},{5,4},{6,5},{7,6},{8,7},{9,8},{10,9},{11,1... | collective-permute-start | bytes 208904 | tf_op jit(solution)/shard_map/ppermute | solution.py:174
  19.7 3.7 %collective-permute-done.19.yu_ref = bf16[272,128]{1,0:T(8,128)(2,1)S(1)} collective-permute-done((bf16[272,128]{1,0:T(8,128)(2,1)S(1)}, bf16[272,128]{1,0:T(8,128)(2,1)S(1)}, u32[]{:S(2)}, u32[]{:S(2)}) %collective-permute-start.19) | collective-permute-done | bytes 69664 | tf_op jit(solution)/shard_map/ppermute | solution.py:174
  23.4 7.1 %forward_conv.3 = (f32[4,512,128]{2,1,0:T(8,128)S(1)}, bf16[4,640,1152]{2,1,0:T(8,128)(2,1)}, f32[8,128]{1,0:T(8,128)S(1)}) custom-call(s32[4,27]{1,0:T(4,128)} %bitcast.46, s32[4,27]{1,0:T(4,128)} %bitcast.47, bf16[4,512,128]{2,1,0:T(8,128)(2,1)S(1)} %get-tuple-element.154.own_ref, bf16[2,64,128]{2,1,0:T(8,128)(2,1)S(1)} %collective-permute-done.16.xl_ref, ...), custom_call_target="tpu_custom_call" | custom-call | flops 6000000000 | bytes 12582912 | tf_op jit(solution)/shard_map/forward_conv/pallas_call | solution.py:304
  30.5 16.1 %all_to_all.57 = f32[16,8,128]{2,1,0:T(8,128)S(1)} all-to-all(f32[16,8,128]{2,1,0:T(8,128)S(1)} %broadcast_in_dim.28), channel_id=1, replica_groups=mesh['xh'=2,'y'=4,'xl'=2,'z'=8,'c'=2] {'z','c'}, dimensions={0} | all-to-all | bytes 131072 | tf_op jit(solution)/shard_map/all_to_all | solution.py:604
  46.6 0.6 broadcast_in_dim.29
  47.3 8.9 %all-to-all-start.11 = ((f32[16,8,128]{2,1,0:T(8,128)}), f32[16,8,128]{2,1,0:T(8,128)}, u32[]{:S(2)}, u32[]{:S(2)}) async-start(f32[16,8,128]{2,1,0:T(8,128)} %broadcast_in_dim.29), calls=%async_computation.11 | async-start | bytes 131072 | tf_op jit(solution)/shard_map/all_to_all | solution.py:604
  56.2 0.0 copy-start.3
  56.2 0.0 copy-start.6
  56.2 0.0 copy-start.9
  56.3 0.0 copy-start.10
  56.3 1.3 reverse_bitcast_fusion
  57.6 1.6 %copy.16 = bf16[27,128,128]{2,1,0:T(8,128)(2,1)} copy(bf16[27,128,128]{1,2,0:T(8,128)(2,1)S(1)} %reverse_bitcast_fusion) | data formatting | bytes 1769472 | tf_op jit(solution)/shard_map/transpose | solution.py:639
  59.2 3.5 %all-to-all-done.11 = f32[16,8,128]{2,1,0:T(8,128)} async-done(((f32[16,8,128]{2,1,0:T(8,128)}), f32[16,8,128]{2,1,0:T(8,128)}, u32[]{:S(2)}, u32[]{:S(2)}) %all-to-all-start.11) | async-done | bytes 65568 | tf_op jit(solution)/shard_map/all_to_all | solution.py:604
  62.8 1.5 slice_reduce_fusion
  64.9 92.4 %conditional.1 = (bf16[4,512,128]{2,1,0:T(8,128)(2,1)}, bf16[4,512,128]{2,1,0:T(8,128)(2,1)}, f32[27,128,128]{2,1,0:T(8,128)S(1)}, f32[1,128]{1,0:T(1,128)}, f32[1,128]{1,0:T(1,128)}) conditional(s32[]{:T(128)} %convert_element_type.3, (bf16[1,1,4,512,128]{4,3,2,1,0:T(8,128)(2,1)S(1)}, f32[16,8,128]{2,1,0:T(8,128)}, f32[4,512,128]{2,1,0:T(8,128)S(1)}, ...), branch_computations={%region_2.0_spmd, %region_3.0_spmd} | conditional | flops 15643816960 | bytes 133288464 | solution.py:668
  65.0 3.0 %activation.2 = (bf16[4,512,128]{2,1,0:T(8,128)(2,1)}, f32[4,512,128]{2,1,0:T(8,128)S(1)}, bf16[4,272,512]{2,1,0:T(8,128)(2,1)S(1)}, f32[8,128]{1,0:T(8,128)S(1)}, f32[8,128]{1,0:T(8,128)S(1)}) custom-call(f32[16,8,128]{2,1,0:T(8,128)} %get-tuple-element.52.stat_ref, f32[4,512,128]{2,1,0:T(8,128)S(1)} %get-tuple-element.53.conv_ref, ...), custom_call_target="tpu_custom_call" | custom-call | flops 8388608 | bytes 5242880 | tf_op jit(solution)/shard_map/cond/branch_0_fun/activation/pallas_call | solution.py:362
  67.9 8.2 %weight_terms.2 = (f32[3632,128]{1,0:T(8,128)S(1)}, bf16[3632,128]{1,0:T(8,128)(2,1)S(1)}) custom-call(s32[1]{0:T(128)} %get-tuple-element.60.core_ref, bf16[4,272,512]{2,1,0:T(8,128)(2,1)S(1)} %get-tuple-element.61.g_ref, bf16[4,640,1152]{2,1,0:T(8,128)(2,1)} %get-tuple-element.62.x9_ref, f32[8,128]{1,0:T(8,128)S(1)} %get-tuple-element.63.sum_ref), custom_call_target="tpu_custom_call" | custom-call | flops 3623878656 | bytes 12582912 | tf_op jit(solution)/shard_map/cond/branch_0_fun/weight_terms/pallas_call | solution.py:448
  76.2 1.7 %collective-permute-start = (bf16[3632,128]{1,0:T(8,128)(2,1)S(1)}, bf16[3632,128]{1,0:T(8,128)(2,1)S(1)}, u32[]{:S(2)}, u32[]{:S(2)}) collective-permute-start(bf16[3632,128]{1,0:T(8,128)(2,1)S(1)} %get-tuple-element.65), channel_id=1, source_target_pairs={{0,1},{1,0},{2,3},{3,2},{4,5},{5,4},{6,7},{7,6},{8,9},{9,8},{10,11... | collective-permute-start | bytes 2789384 | tf_op jit(solution)/shard_map/cond/branch_0_fun/ppermute | solution.py:612
  77.8 2.1 %collective-permute-done.got_ref = bf16[3632,128]{1,0:T(8,128)(2,1)S(1)} collective-permute-done((bf16[3632,128]{1,0:T(8,128)(2,1)S(1)}, bf16[3632,128]{1,0:T(8,128)(2,1)S(1)}, u32[]{:S(2)}, u32[]{:S(2)}) %collective-permute-start) | collective-permute-done | bytes 929824 | tf_op jit(solution)/shard_map/cond/branch_0_fun/ppermute | solution.py:612
  80.0 0.2 join.2
  80.2 20.1 %all_to_all.50.parts_ref = bf16[16,272,128]{2,1,0:T(8,128)(2,1)S(1)} all-to-all(bf16[16,272,128]{2,1,0:T(8,128)(2,1)S(1)} %join.2), channel_id=1, replica_groups=mesh['xh'=2,'y'=4,'xl'=2,'z'=8,'c'=2] {'xh','y','xl'}, dimensions={0} | all-to-all | bytes 2228224 | tf_op jit(solution)/shard_map/cond/branch_0_fun/all_to_all | solution.py:650
  100.3 0.2 middle.2
  100.4 10.8 %all_to_all.51.parts_ref = f32[8,40,128]{2,1,0:T(8,128)S(1)} all-to-all(f32[8,40,128]{2,1,0:T(8,128)S(1)} %middle.2), channel_id=1, replica_groups=mesh['xh'=2,'y'=4,'xl'=2,'z'=8,'c'=2] {'z'}, dimensions={0} | all-to-all | bytes 327680 | tf_op jit(solution)/shard_map/cond/branch_0_fun/all_to_all | solution.py:651
  111.2 0.5 combine.2
  111.7 1.1 grad_conv.2
  112.8 0.6 broadcast_in_dim.6
  113.4 3.3 %all-to-all-start.2 = ((bf16[8,16,128]{2,1,0:T(8,128)(2,1)}), bf16[8,16,128]{2,1,0:T(8,128)(2,1)S(1)}, u32[]{:S(2)}, u32[]{:S(2)}) async-start(bf16[8,16,128]{2,1,0:T(8,128)(2,1)} %broadcast_in_dim.6), calls=%async_computation.2 | async-start | bytes 65536 | tf_op jit(solution)/shard_map/cond/branch_0_fun/all_to_all | solution.py:604
  116.8 1.8 %collective-permute-start.1 = (bf16[2,64,128]{2,1,0:T(8,128)(2,1)S(1)}, bf16[2,64,128]{2,1,0:T(8,128)(2,1)S(1)}, u32[]{:S(2)}, u32[]{:S(2)}) collective-permute-start(bf16[2,64,128]{2,1,0:T(8,128)(2,1)S(1)} %get-tuple-element.76), channel_id=1, source_target_pairs={{0,32},{32,64},{64,96},{96,128},{128,160},{160,192},{192,224},{1,3... | collective-permute-start | bytes 98312 | tf_op jit(solution)/shard_map/cond/branch_0_fun/ppermute | solution.py:174
  118.6 1.3 collective-permute-start.2
  119.9 3.6 %collective-permute-done.2.xu_ref = bf16[2,64,128]{2,1,0:T(8,128)(2,1)S(1)} collective-permute-done((bf16[2,64,128]{2,1,0:T(8,128)(2,1)S(1)}, bf16[2,64,128]{2,1,0:T(8,128)(2,1)S(1)}, u32[]{:S(2)}, u32[]{:S(2)}) %collective-permute-start.2) | collective-permute-done | bytes 32800 | tf_op jit(solution)/shard_map/cond/branch_0_fun/ppermute | solution.py:174
  123.6 0.7 pick_y.4
  124.3 7.5 %collective-permute-start.3 = (bf16[272,128]{1,0:T(8,128)(2,1)S(1)}, bf16[272,128]{1,0:T(8,128)(2,1)S(1)}, u32[]{:S(2)}, u32[]{:S(2)}) collective-permute-start(bf16[272,128]{1,0:T(8,128)(2,1)S(1)} %get-tuple-element.82), channel_id=1, source_target_pairs={{0,1},{1,2},{2,3},{3,4},{4,5},{5,6},{6,7},{7,8},{8,9},{9,10},{10,1... | collective-permute-start | bytes 208904 | tf_op jit(solution)/shard_map/cond/branch_0_fun/ppermute | solution.py:174
  131.9 1.9 %collective-permute-start.4 = (bf16[272,128]{1,0:T(8,128)(2,1)S(1)}, bf16[272,128]{1,0:T(8,128)(2,1)S(1)}, u32[]{:S(2)}, u32[]{:S(2)}) collective-permute-start(bf16[272,128]{1,0:T(8,128)(2,1)S(1)} %get-tuple-element.83), channel_id=1, source_target_pairs={{1,0},{2,1},{3,2},{4,3},{5,4},{6,5},{7,6},{8,7},{9,8},{10,9},{11,1... | collective-permute-start | bytes 208904 | tf_op jit(solution)/shard_map/cond/branch_0_fun/ppermute | solution.py:174
  133.8 0.8 broadcast_in_dim.7
  134.6 8.3 %all-to-all-start.3 = ((bf16[16,112,128]{2,1,0:T(8,128)(2,1)}), bf16[16,112,128]{2,1,0:T(8,128)(2,1)S(1)}, u32[]{:S(2)}, u32[]{:S(2)}) async-start(bf16[16,112,128]{2,1,0:T(8,128)(2,1)} %broadcast_in_dim.7), calls=%async_computation.3 | async-start | bytes 917504 | tf_op jit(solution)/shard_map/cond/branch_0_fun/all_to_all | solution.py:604
  143.0 6.0 %transposed_conv.2 = bf16[4,512,128]{2,1,0:T(8,128)(2,1)} custom-call(s32[4,27]{1,0:T(4,128)S(1)} %get-tuple-element.81.map_ref.rows_ref, s32[4,27]{1,0:T(4,128)S(1)} %get-tuple-element.81.map_ref.rows_ref, bf16[4,512,128]{2,1,0:T(8,128)(2,1)S(1)} %get-tuple-element.75.own_ref, bf16[2,64,128]{2,1,0:T(8,128)(2,1)S(1)} %collective-permute-done.1.xl_ref, ...), custom_call_target="tpu_custom_call" | custom-call | flops 6000000000 | bytes 12582912 | tf_op jit(solution)/shard_map/cond/branch_0_fun/transposed_conv/pallas_call | solution.py:304
  149.1 2.5 %all-to-all-done.3.mine_ref = bf16[16,112,128]{2,1,0:T(8,128)(2,1)S(1)} async-done(((bf16[16,112,128]{2,1,0:T(8,128)(2,1)}), bf16[16,112,128]{2,1,0:T(8,128)(2,1)S(1)}, u32[]{:S(2)}, u32[]{:S(2)}) %all-to-all-start.3) | async-done | bytes 458784 | tf_op jit(solution)/shard_map/cond/branch_0_fun/all_to_all | solution.py:604
  151.6 3.8 %collective-permute-start.5 = (bf16[16,112,128]{2,1,0:T(8,128)(2,1)S(1)}, bf16[16,112,128]{2,1,0:T(8,128)(2,1)S(1)}, u32[]{:S(2)}, u32[]{:S(2)}) collective-permute-start(bf16[16,112,128]{2,1,0:T(8,128)(2,1)S(1)} %all-to-all-done.3.mine_ref), channel_id=1, source_target_pairs={{0,1},{1,0},{2,3},{3,2},{4,5},{5,4},{6,7},{7,6},{8,9},{9,8},{10,11... | collective-permute-start | bytes 1376264 | tf_op jit(solution)/shard_map/cond/branch_0_fun/ppermute | solution.py:612
  155.3 1.4 collective-permute-done.5.other_ref
  156.8 0.3 finish.2
  157.3 0.0 copy-start.4
  157.3 1.2 copy-done.4
  (23 shorter events, 0.1 us)
Async XLA Ops:
  2.7 5.3 %collective-permute-start.16 = (bf16[2,64,128]{2,1,0:T(8,128)(2,1)S(1)}, bf16[2,64,128]{2,1,0:T(8,128)(2,1)S(1)}, u32[]{:S(2)}, u32[]{:S(2)}) collective-permute-start(bf16[2,64,128]{2,1,0:T(8,128)(2,1)S(1)} %get-tuple-element.155), channel_id=1, source_target_pairs={{0,32},{32,64},{64,96},{96,128},{128,160},{160,192},{192,224},{1,3... | collective-permute-start | bytes 98312 | tf_op jit(solution)/shard_map/ppermute | solution.py:174
  6.7 4.7 %collective-permute-start.17 = (bf16[2,64,128]{2,1,0:T(8,128)(2,1)S(1)}, bf16[2,64,128]{2,1,0:T(8,128)(2,1)S(1)}, u32[]{:S(2)}, u32[]{:S(2)}) collective-permute-start(bf16[2,64,128]{2,1,0:T(8,128)(2,1)S(1)} %get-tuple-element.156), channel_id=1, source_target_pairs={{32,0},{64,32},{96,64},{128,96},{160,128},{192,160},{224,192},{33,... | collective-permute-start | bytes 98312 | tf_op jit(solution)/shard_map/ppermute | solution.py:174
  12.3 7.5 %collective-permute-start.18 = (bf16[272,128]{1,0:T(8,128)(2,1)S(1)}, bf16[272,128]{1,0:T(8,128)(2,1)S(1)}, u32[]{:S(2)}, u32[]{:S(2)}) collective-permute-start(bf16[272,128]{1,0:T(8,128)(2,1)S(1)} %get-tuple-element.157), channel_id=1, source_target_pairs={{0,1},{1,2},{2,3},{3,4},{4,5},{5,6},{6,7},{7,8},{8,9},{9,10},{10,1... | collective-permute-start | bytes 208904 | tf_op jit(solution)/shard_map/ppermute | solution.py:174
  17.8 5.6 %collective-permute-start.19 = (bf16[272,128]{1,0:T(8,128)(2,1)S(1)}, bf16[272,128]{1,0:T(8,128)(2,1)S(1)}, u32[]{:S(2)}, u32[]{:S(2)}) collective-permute-start(bf16[272,128]{1,0:T(8,128)(2,1)S(1)} %get-tuple-element.158), channel_id=1, source_target_pairs={{1,0},{2,1},{3,2},{4,3},{5,4},{6,5},{7,6},{8,7},{9,8},{10,9},{11,1... | collective-permute-start | bytes 208904 | tf_op jit(solution)/shard_map/ppermute | solution.py:174
  47.3 15.5 %all-to-all-start.11 = ((f32[16,8,128]{2,1,0:T(8,128)}), f32[16,8,128]{2,1,0:T(8,128)}, u32[]{:S(2)}, u32[]{:S(2)}) async-start(f32[16,8,128]{2,1,0:T(8,128)} %broadcast_in_dim.29), calls=%async_computation.11 | async-start | bytes 131072 | tf_op jit(solution)/shard_map/all_to_all | solution.py:604
  56.2 8.7 %copy-start.2 = (bf16[1,1,4,512,128]{4,3,2,1,0:T(8,128)(2,1)S(1)}, bf16[1,1,4,512,128]{4,3,2,1,0:T(8,128)(2,1)}, u32[]{:S(2)}) copy-start(bf16[1,1,4,512,128]{4,3,2,1,0:T(8,128)(2,1)} %param.12) | copy-start | bytes 1572868
  56.2 8.7 %copy-start.3 = (bf16[1,1,4,512,128]{4,3,2,1,0:T(8,128)(2,1)S(1)}, bf16[1,1,4,512,128]{4,3,2,1,0:T(8,128)(2,1)}, u32[]{:S(2)}) copy-start(bf16[1,1,4,512,128]{4,3,2,1,0:T(8,128)(2,1)} %param.21) | copy-start | bytes 1572868
  56.2 8.7 %copy-start.6 = (s32[1,1,4,512]{3,2,1,0:T(4,128)S(1)}, s32[1,1,4,512]{3,2,1,0:T(4,128)}, u32[]{:S(2)}) copy-start(s32[1,1,4,512]{3,2,1,0:T(4,128)} %param.13) | copy-start | bytes 24580
  56.2 8.7 %copy-start.7 = (f32[128]{0:T(128)S(1)}, f32[128]{0:T(128)}, u32[]{:S(2)}) copy-start(f32[128]{0:T(128)} %param.19) | copy-start | bytes 1540
  56.2 8.7 %copy-start.8 = (s32[1,1,2,2]{3,2,1,0:T(2,128)S(1)}, s32[1,1,2,2]{3,2,1,0:T(2,128)}, u32[]{:S(2)}) copy-start(s32[1,1,2,2]{3,2,1,0:T(2,128)} %param.16) | copy-start | bytes 52
  56.2 8.7 %copy-start.9 = (s32[1,1,2,4]{3,2,1,0:T(2,128)S(1)}, s32[1,1,2,4]{3,2,1,0:T(2,128)}, u32[]{:S(2)}) copy-start(s32[1,1,2,4]{3,2,1,0:T(2,128)} %param.17) | copy-start | bytes 100
  56.3 8.7 %copy-start.10 = (f32[128]{0:T(128)S(1)}, f32[128]{0:T(128)}, u32[]{:S(2)}) copy-start(f32[128]{0:T(128)} %param.20) | copy-start | bytes 1540
  56.3 8.7 %copy-start.11 = (s32[1,1,4,27]{3,2,1,0:T(4,128)S(1)}, s32[1,1,4,27]{3,2,1,0:T(4,128)}, u32[]{:S(2)}) copy-start(s32[1,1,4,27]{3,2,1,0:T(4,128)} %param.15) | copy-start | bytes 1300
  76.2 3.8 %collective-permute-start = (bf16[3632,128]{1,0:T(8,128)(2,1)S(1)}, bf16[3632,128]{1,0:T(8,128)(2,1)S(1)}, u32[]{:S(2)}, u32[]{:S(2)}) collective-permute-start(bf16[3632,128]{1,0:T(8,128)(2,1)S(1)} %get-tuple-element.65), channel_id=1, source_target_pairs={{0,1},{1,0},{2,3},{3,2},{4,5},{5,4},{6,7},{7,6},{8,9},{9,8},{10,11... | collective-permute-start | bytes 2789384 | tf_op jit(solution)/shard_map/cond/branch_0_fun/ppermute | solution.py:612
  112.8 30.2 %copy-start.5 = (bf16[3,1152,128]{2,1,0:T(8,128)(2,1)S(1)}, bf16[3,1152,128]{2,1,0:T(8,128)(2,1)}, u32[]{:S(2)}) copy-start(bf16[3,1152,128]{2,1,0:T(8,128)(2,1)} %get-tuple-element.84.w_ref) | copy-start | bytes 2654212 | tf_op jit(solution)/shard_map/cond
  113.4 10.9 %all-to-all-start.2 = ((bf16[8,16,128]{2,1,0:T(8,128)(2,1)}), bf16[8,16,128]{2,1,0:T(8,128)(2,1)S(1)}, u32[]{:S(2)}, u32[]{:S(2)}) async-start(bf16[8,16,128]{2,1,0:T(8,128)(2,1)} %broadcast_in_dim.6), calls=%async_computation.2 | async-start | bytes 65536 | tf_op jit(solution)/shard_map/cond/branch_0_fun/all_to_all | solution.py:604
  116.8 3.1 %collective-permute-start.1 = (bf16[2,64,128]{2,1,0:T(8,128)(2,1)S(1)}, bf16[2,64,128]{2,1,0:T(8,128)(2,1)S(1)}, u32[]{:S(2)}, u32[]{:S(2)}) collective-permute-start(bf16[2,64,128]{2,1,0:T(8,128)(2,1)S(1)} %get-tuple-element.76), channel_id=1, source_target_pairs={{0,32},{32,64},{64,96},{96,128},{128,160},{160,192},{192,224},{1,3... | collective-permute-start | bytes 98312 | tf_op jit(solution)/shard_map/cond/branch_0_fun/ppermute | solution.py:174
  118.6 5.0 %collective-permute-start.2 = (bf16[2,64,128]{2,1,0:T(8,128)(2,1)S(1)}, bf16[2,64,128]{2,1,0:T(8,128)(2,1)S(1)}, u32[]{:S(2)}, u32[]{:S(2)}) collective-permute-start(bf16[2,64,128]{2,1,0:T(8,128)(2,1)S(1)} %get-tuple-element.77), channel_id=1, source_target_pairs={{32,0},{64,32},{96,64},{128,96},{160,128},{192,160},{224,192},{33,... | collective-permute-start | bytes 98312 | tf_op jit(solution)/shard_map/cond/branch_0_fun/ppermute | solution.py:174
  124.3 18.7 %collective-permute-start.3 = (bf16[272,128]{1,0:T(8,128)(2,1)S(1)}, bf16[272,128]{1,0:T(8,128)(2,1)S(1)}, u32[]{:S(2)}, u32[]{:S(2)}) collective-permute-start(bf16[272,128]{1,0:T(8,128)(2,1)S(1)} %get-tuple-element.82), channel_id=1, source_target_pairs={{0,1},{1,2},{2,3},{3,4},{4,5},{5,6},{6,7},{7,8},{8,9},{9,10},{10,1... | collective-permute-start | bytes 208904 | tf_op jit(solution)/shard_map/cond/branch_0_fun/ppermute | solution.py:174
  131.9 11.1 %collective-permute-start.4 = (bf16[272,128]{1,0:T(8,128)(2,1)S(1)}, bf16[272,128]{1,0:T(8,128)(2,1)S(1)}, u32[]{:S(2)}, u32[]{:S(2)}) collective-permute-start(bf16[272,128]{1,0:T(8,128)(2,1)S(1)} %get-tuple-element.83), channel_id=1, source_target_pairs={{1,0},{2,1},{3,2},{4,3},{5,4},{6,5},{7,6},{8,7},{9,8},{10,9},{11,1... | collective-permute-start | bytes 208904 | tf_op jit(solution)/shard_map/cond/branch_0_fun/ppermute | solution.py:174
  134.6 16.9 %all-to-all-start.3 = ((bf16[16,112,128]{2,1,0:T(8,128)(2,1)}), bf16[16,112,128]{2,1,0:T(8,128)(2,1)S(1)}, u32[]{:S(2)}, u32[]{:S(2)}) async-start(bf16[16,112,128]{2,1,0:T(8,128)(2,1)} %broadcast_in_dim.7), calls=%async_computation.3 | async-start | bytes 917504 | tf_op jit(solution)/shard_map/cond/branch_0_fun/all_to_all | solution.py:604
  151.6 5.2 %collective-permute-start.5 = (bf16[16,112,128]{2,1,0:T(8,128)(2,1)S(1)}, bf16[16,112,128]{2,1,0:T(8,128)(2,1)S(1)}, u32[]{:S(2)}, u32[]{:S(2)}) collective-permute-start(bf16[16,112,128]{2,1,0:T(8,128)(2,1)S(1)} %all-to-all-done.3.mine_ref), channel_id=1, source_target_pairs={{0,1},{1,0},{2,3},{3,2},{4,5},{5,4},{6,7},{7,6},{8,9},{9,8},{10,11... | collective-permute-start | bytes 1376264 | tf_op jit(solution)/shard_map/cond/branch_0_fun/ppermute | solution.py:612
  157.3 1.2 copy-start.4
